TPU v7x, 256 devices: a whole 4x4x8 slice. The times are simulated.
256 devices in a mesh: sect: 4 (over z_hi), ctx: 8 (over z_lo, y), tp: 8 (over x, core).
Axes of the slice: x: 4, y: 4, z: 8 (z_hi: 4, z_lo: 2; z = z_hi * 2 + z_lo), core: 2. Of those that a mesh axis runs over, the one named last changes fastest.
Arguments:
- patches: bfloat16 [4096, 1280], P(('sect', 'ctx')), may hold values from -6 to 6
- patch_gain: float32 [1280], replicated, may hold values from 0.25 to 1.75
- patch_shift: float32 [1280], replicated, may hold values from -3 to 3
- encoder_up: bfloat16 [1280, 5120], P(None, 'tp'), may hold values from -0.15625 to 0.15625
- encoder_down: bfloat16 [5120, 1280], P('tp'), may hold values from -0.078125 to 0.078125
- proj_weight: bfloat16 [1280, 8192], P(None, 'tp'), may hold values from -0.15625 to 0.15625
- hidden_text: bfloat16 [8192, 8192], P(('sect', 'ctx'), 'tp'), may hold values from -180 to 180
- slot_source: int32 [64], P(('sect', 'ctx')), may hold values from 0 to 4, as said below
- norm_gain: float32 [8192], P('tp'), may hold values from 0.25 to 1.75
- kv_weight: bfloat16 [2048, 8192], P(None, 'tp'), may hold values from -0.0625 to 0.0625
- queries: bfloat16 [8192, 4096], P(('sect', 'ctx'), 'tp'), may hold values from -40 to 40
Outputs:
- attended: bfloat16 [8192, 4096], P(('sect', 'ctx'), 'tp')
Inputs may be any that keep to these rules, and one draw needn't show every extreme that they name: `slot_source`: for each ctx index, the slots of the blocks with that index carry each value 0 to 3 exactly once, all other slots 4.
All inputs are finite; a program needn't handle non-finite values.
Results may differ from a plain program's by a relative error of at most 0.019.
Values may be sent and summed in bfloat16 or wider, within the bound.
No kernel may reach another device: no remote copies, remote signals or barrier semaphores. Data moves between devices by JAX's collectives and lax.ppermute only.
A program may use at most 128 MiB of HBM per device.

v0:
```python
import functools
import math

import jax
import jax.numpy as jnp
from jax import lax
from jax.experimental import pallas as pl
from jax.experimental.pallas import tpu as pltpu
from jax.sharding import Mesh
from jax.sharding import PartitionSpec as P

D = 8192
HEAD = 128
HALF = 64
GROUP = 4
TOK = 256
IMG = 128
ROWS = 272
TP = ("x", "core")
Z = ("zh", "zl")
BF16 = jnp.bfloat16
F32 = jnp.float32
NEG = -1e30
LOG2E = math.log2(math.e)
WIDE = TOK + IMG
KEYS = 2048
CHUNK = 1024
PER = CHUNK // TOK
ROWS_Q = GROUP * TOK
SCALE = HEAD ** (-0.5)


def shift(values, axis, step):
    count = lax.axis_size(axis)
    return lax.ppermute(values, axis, [(i, (i + step) % count) for i in range(count)])


def pick(values, index):
    return lax.dynamic_index_in_dim(values, index, 0, keepdims=False)


def vmem(mib):
    return pltpu.CompilerParams(vmem_limit_bytes=mib * 1024 * 1024)


def split_squares(column, count):
    row = jnp.broadcast_to(column, (count, HEAD)).T[:16]
    high = row.astype(BF16).astype(F32)
    at = lax.broadcasted_iota(jnp.int32, row.shape, 0)
    return jnp.where(at == 0, high, jnp.where(at == 1, row - high, 0.0)).astype(BF16)


def head_rows(core, features, tail, weight_ref, give_ref, keep_ref):
    @pl.loop(0, 4)
    def one_chip(x_at):
        for own, ref in ((0, give_ref), (1, keep_ref)):
            head = 2 * x_at + jnp.where(own == 1, core, 1 - core)
            weight = weight_ref[pl.ds(pl.multiple_of(head * TOK, TOK), TOK), :]
            rows = lax.dot_general(
                weight, features, (((1,), (1,)), ((), ())), preferred_element_type=F32
            )
            ref[x_at, :TOK, :] = rows.astype(BF16)
            ref[x_at, TOK:, :] = tail


def gain_features(features, gain_ref):
    widened = features.astype(F32)
    squares = jnp.sum(jnp.square(widened), axis=1, keepdims=True)
    return (widened * gain_ref[...]).astype(BF16), split_squares(squares, features.shape[0])


def text_project_kernel(core, hidden_ref, gain_ref, weight_ref, give_ref, keep_ref):
    gained, tail = gain_features(hidden_ref[...], gain_ref)
    head_rows(core[0], gained, tail, weight_ref, give_ref, keep_ref)


def image_project_kernel(
    core, half_ref, other_ref, proj_ref, gain_ref, weight_ref, give_ref, keep_ref, encoded
):
    at = pl.multiple_of(core[0] * HALF, HALF)
    encoded[pl.ds(at, HALF), :] = half_ref[...]
    encoded[pl.ds(HALF - at, HALF), :] = other_ref[...]
    image = jnp.dot(encoded[...], proj_ref[...], preferred_element_type=F32).astype(BF16)
    gained, tail = gain_features(image, gain_ref)
    head_rows(core[0], gained, tail, weight_ref, give_ref, keep_ref)


def project(kernel, features, norm_gain, kv_weight, core, count, scratch):
    mine = jnp.reshape(core, (1,)).astype(jnp.int32)
    shape = jax.ShapeDtypeStruct((4, ROWS, count), BF16)
    return pl.pallas_call(
        kernel,
        out_shape=(shape, shape),
        in_specs=[
            pl.BlockSpec(memory_space=pltpu.SMEM),
            *[pl.BlockSpec(memory_space=pltpu.VMEM)] * (len(features) + 2),
        ],
        scratch_shapes=scratch,
        compiler_params=vmem(8),
        name="project",
    )(mine, *features, norm_gain[None, :], kv_weight)


def pair_kernel(place, keep_ref, got_ref, own_ref, two_ref, one_ref, three_ref):
    for step, ref in ((2, two_ref), (1, one_ref), (3, three_ref), (0, own_ref)):
        at = lax.rem(place[0] + step, 4)
        total = keep_ref[at].astype(F32) + got_ref[at].astype(F32)
        ref[...] = total.astype(ref.dtype)


def add_pair(keep, got, x_at):
    part = keep.shape[1:]
    return pl.pallas_call(
        pair_kernel,
        out_shape=(jax.ShapeDtypeStruct(part, F32), *[jax.ShapeDtypeStruct(part, BF16)] * 3),
        in_specs=[
            pl.BlockSpec(memory_space=pltpu.SMEM),
            *[pl.BlockSpec(memory_space=pltpu.VMEM)] * 2,
        ],
        compiler_params=vmem(6),
        name="add_pair",
    )(jnp.reshape(x_at, (1,)).astype(jnp.int32), keep, got)


def finish_kernel(slots, *refs):
    *inputs, out_ref = refs
    for lanes, pieces in ((slice(0, TOK), inputs[:4]), (slice(TOK, WIDE), inputs[4:])):
        total = pieces[0][...]
        for ref in pieces[1:]:
            total = total + ref[...].astype(F32)
        inverse = lax.rsqrt((total[TOK : TOK + 1] + total[TOK + 1 : TOK + 2]) / D + 1e-05)
        out_ref[:TOK, lanes] = (total[:TOK] * inverse).astype(BF16)
    lane = lax.broadcasted_iota(jnp.int32, (ROWS - TOK, WIDE), 1)
    out_ref[TOK:, :] = jnp.where(lane < IMG, slots[0], slots[1]).astype(F32).astype(BF16)


def finish_rows(slots, text, image):
    return pl.pallas_call(
        finish_kernel,
        out_shape=jax.ShapeDtypeStruct((ROWS, WIDE), BF16),
        in_specs=[
            pl.BlockSpec(memory_space=pltpu.SMEM),
            *[pl.BlockSpec(memory_space=pltpu.VMEM)] * 8,
        ],
        compiler_params=vmem(6),
        name="finish_rows",
    )(slots, *text, *image)


def ring_gather(block):
    blocks, up, down = [block], block, block
    for _ in range(3):
        up, down = shift(up, Z, 1), shift(down, Z, 7)
        blocks += [up, down]
    return [*blocks, shift(up[:IMG], Z, 1), shift(down[IMG:], Z, 7)]


def exchange(pieces):
    own, two, one, three = pieces
    return [own, shift(two, "x", 2), shift(one, "x", 1), shift(three, "x", 3)]


def merge_kernel(place, *refs):
    *blocks, cos_ref, sin_ref, outer_cos_ref, outer_sin_ref, keys, values, gathered = refs
    for step, ref in zip((0, 7, 1, 6, 2, 5, 3), blocks):
        gathered[lax.rem(place[0] + step, 8)] = ref[...]
    far = lax.rem(place[0] + 4, 8)
    gathered[far, :IMG, :] = blocks[7][...]
    gathered[far, IMG:, :] = blocks[8][...]
    values[:, HEAD:] = jnp.ones((KEYS, HEAD), BF16)

    @pl.loop(0, 8)
    def one_block(block):
        outer_cos, outer_sin = outer_cos_ref[block], outer_sin_ref[block]
        for slot in range(2):
            lanes = slice(slot * IMG, (slot + 1) * IMG)
            here = pl.ds(pl.multiple_of(block * TOK + slot * IMG, IMG), IMG)
            text = gathered[block, :, lanes].astype(F32)
            source = text[TOK : TOK + 1, :]
            rows = text[:TOK, :]
            for r in range(4):
                image = gathered[2 * r + lax.rem(block, 2), :TOK, TOK:]
                rows = jnp.where(source == float(r), image.astype(F32), rows)
            inner_cos, inner_sin = cos_ref[:, lanes], sin_ref[:, lanes]
            cosine = inner_cos * outer_cos - inner_sin * outer_sin
            sine = inner_sin * outer_cos + inner_cos * outer_sin
            first, second = rows[:HALF], rows[HALF:HEAD]
            keys[:HALF, here] = (first * cosine - second * sine).astype(BF16)
            keys[HALF:, here] = (second * cosine + first * sine).astype(BF16)
            values[here, :HEAD] = rows[HEAD:].T.astype(BF16)


def merge(place, blocks, tables):
    return pl.pallas_call(
        merge_kernel,
        out_shape=(
            jax.ShapeDtypeStruct((HEAD, KEYS), BF16),
            jax.ShapeDtypeStruct((KEYS, 2 * HEAD), BF16),
        ),
        in_specs=[
            pl.BlockSpec(memory_space=pltpu.SMEM),
            *[pl.BlockSpec(memory_space=pltpu.VMEM)] * (len(blocks) + len(tables)),
        ],
        scratch_shapes=[pltpu.VMEM((8, ROWS, WIDE), BF16)],
        compiler_params=vmem(10),
        name="merge",
    )(place, *blocks, *tables)


def attend_kernel(step, place, keys, values, query_ref, out_ref, scores, top, mixed):
    z_at, y_at = place[0], place[1]
    block_at = lax.rem(y_at + step, 4)
    count = z_at + jnp.where(y_at <= block_at, 1, 0)
    chunks = (count + PER - 1) // PER
    top[...] = jnp.full(top.shape, NEG, F32)

    def chunk_at(chunk, offset=0, size=CHUNK):
        return pl.ds(pl.multiple_of(chunk * CHUNK + offset, HEAD), size)

    key_at = lax.broadcasted_iota(jnp.int32, (TOK, CHUNK), 1)
    reach = lax.broadcasted_iota(jnp.int32, (TOK, CHUNK), 0) - key_at - (key_at // TOK) * (3 * TOK)

    @pl.loop(0, chunks)
    def score(chunk):
        keys_now = keys[:, chunk_at(chunk)]
        allowed = reach >= ((PER * chunk - z_at) * 4 + y_at - block_at) * TOK
        for h in range(GROUP):
            here = slice(h * TOK, (h + 1) * TOK)
            s = jnp.dot(
                query_ref[:, h * HEAD : (h + 1) * HEAD], keys_now, preferred_element_type=F32
            )
            s = jnp.where(allowed, s, -jnp.inf)
            scores[here, chunk_at(chunk)] = s
            most = top[here, :]
            for lane in range(0, CHUNK, HEAD):
                most = jnp.maximum(most, s[:, lane : lane + HEAD])
            top[here, :] = most

    top[...] = jnp.broadcast_to(jnp.max(top[...], axis=1, keepdims=True), top.shape)

    mixed[...] = jnp.zeros(mixed.shape, F32)

    @pl.loop(0, chunks)
    def weigh(chunk):
        values_now = values[chunk_at(chunk), :]
        for h in range(GROUP):
            here = slice(h * TOK, (h + 1) * TOK)
            most = top[here, :]
            weights = jnp.concatenate(
                [
                    jnp.exp2(scores[here, chunk_at(chunk, lane, HEAD)] - most).astype(BF16)
                    for lane in range(0, CHUNK, HEAD)
                ],
                1,
            )
            rows = jnp.dot(weights, values_now, preferred_element_type=F32)
            mixed[here, :] += rows

    lane = lax.broadcasted_iota(jnp.int32, (TOK, HEAD), 1)
    stats = jnp.zeros((TOK, HEAD), F32)
    for h in range(GROUP):
        here = slice(h * TOK, (h + 1) * TOK)
        total = mixed[here, HEAD:]
        safe = jnp.where(total > 0.0, total, 1.0)
        out_ref[:TOK, h * HEAD : (h + 1) * HEAD] = (mixed[here, :HEAD] / safe).astype(BF16)
        stats = jnp.where(lane == h, top[here, :], jnp.where(lane == GROUP + h, total, stats))
    rows = stats.T
    tops, totals = rows[:GROUP], rows[GROUP : 2 * GROUP]
    some = totals > 0.0
    level = jnp.where(some, tops + jnp.log2(jnp.where(some, totals, 1.0)), NEG)
    high = level.astype(BF16).astype(F32)
    middle = (level - high).astype(BF16).astype(F32)
    low = level - high - middle
    pad = jnp.zeros((ROWS - TOK - 3 * GROUP, TOK), F32)
    out_ref[TOK:, :TOK] = jnp.concatenate([high, middle, low, pad], 0).astype(BF16)
    out_ref[TOK:, TOK:] = jnp.zeros((ROWS - TOK, 2 * HEAD), BF16)


def attend(step, place, keys, values, queries):
    return pl.pallas_call(
        functools.partial(attend_kernel, step),
        out_shape=jax.ShapeDtypeStruct((ROWS, GROUP * HEAD), BF16),
        in_specs=[
            pl.BlockSpec(memory_space=pltpu.SMEM),
            *[pl.BlockSpec(memory_space=pltpu.VMEM)] * 3,
        ],
        scratch_shapes=[
            pltpu.VMEM((ROWS_Q, KEYS), F32),
            pltpu.VMEM((ROWS_Q, HEAD), F32),
            pltpu.VMEM((ROWS_Q, 2 * HEAD), F32),
        ],
        compiler_params=vmem(24),
        cost_estimate=pl.CostEstimate(
            flops=4 * ROWS_Q * KEYS * HEAD, bytes_accessed=2 << 20, transcendentals=ROWS_Q * KEYS
        ),
        name="attend",
    )(place, keys, values, queries)


def layer_norm(values, norm_scale, norm_shift):
    widened = values.astype(F32)
    center = jnp.mean(widened, axis=-1, keepdims=True)
    spread = jnp.mean(jnp.square(widened - center), axis=-1, keepdims=True)
    return ((widened - center) * lax.rsqrt(spread + 1e-06) * norm_scale + norm_shift).astype(BF16)


def combine_kernel(*refs):
    *parts, out_ref = refs
    levels = []
    for ref in parts:
        rows = ref[TOK:, :TOK].astype(F32)
        levels.append(
            [rows[h : h + 1] + rows[4 + h : 5 + h] + rows[8 + h : 9 + h] for h in range(GROUP)]
        )
    weights = []
    for h in range(GROUP):
        most = functools.reduce(jnp.maximum, [level[h] for level in levels])
        raised = [jnp.exp2(level[h] - most) for level in levels]
        total = sum(raised)
        weights += [r / total for r in raised]
    rows = jnp.concatenate([*weights, jnp.zeros((HEAD - len(weights), TOK), F32)], 0).T
    for h in range(GROUP):
        lanes = slice(h * HEAD, (h + 1) * HEAD)
        mixed = sum(
            rows[:, 4 * h + i : 4 * h + i + 1] * ref[:TOK, lanes].astype(F32)
            for i, ref in enumerate(parts)
        )
        out_ref[:, lanes] = mixed.astype(BF16)


def combine(parts):
    return pl.pallas_call(
        combine_kernel,
        out_shape=jax.ShapeDtypeStruct((TOK, GROUP * HEAD), BF16),
        compiler_params=vmem(6),
        name="combine",
    )(*parts)


def body(
    patches,
    patch_gain,
    patch_shift,
    encoder_up,
    encoder_down,
    proj_weight,
    hidden_text,
    slot_source,
    norm_gain,
    kv_weight,
    queries,
):
    z_at, y_at = lax.axis_index(Z), lax.axis_index("y")
    x_at, core = lax.axis_index("x"), lax.axis_index("core")

    place = jnp.stack([z_at, y_at]).astype(jnp.int32)

    normed_patches = layer_norm(patches, patch_gain, patch_shift)
    enc_hidden = jax.nn.gelu(
        jnp.dot(normed_patches, encoder_up, preferred_element_type=F32), approximate=False
    ).astype(BF16)
    partial_out = jnp.dot(enc_hidden, encoder_down, preferred_element_type=F32).astype(BF16)
    halves = partial_out.reshape(2, HALF, -1)
    half = pick(halves, core).astype(F32) + shift(pick(halves, 1 - core), "core", 1).astype(F32)
    sent = half.astype(BF16)
    sent, hidden_text = lax.optimization_barrier((sent, hidden_text))

    give, keep = project(text_project_kernel, [hidden_text], norm_gain, kv_weight, core, TOK, [])
    text_pieces = add_pair(keep, shift(give, "core", 1), x_at)
    for step in (2, 1, 3):
        half = half + shift(sent, "x", step).astype(F32)
    half = (half + pick(patches.reshape(2, HALF, -1), core).astype(F32)).astype(BF16)
    half, text_pieces = lax.optimization_barrier((half, text_pieces))
    text_got = exchange(text_pieces)
    other = shift(half, "core", 1)

    give, keep = project(
        image_project_kernel,
        [half, other, proj_weight],
        norm_gain,
        kv_weight,
        core,
        IMG,
        [pltpu.VMEM(patches.shape, BF16)],
    )
    give, keep, text_got = lax.optimization_barrier((give, keep, text_got))
    image_got = exchange(add_pair(keep, shift(give, "core", 1), x_at))
    blocks = ring_gather(finish_rows(slot_source, text_got, image_got))
    asked = {step: shift(queries, "y", 4 - step) for step in (2, 1, 3)}

    frequencies = jnp.exp(
        jnp.arange(HALF, dtype=F32) * (-2.0 * math.log(500000.0) / (2 * HALF))
    )
    inner = jnp.arange(TOK, dtype=F32)[None, :] * frequencies[:, None]
    starts = ((jnp.arange(8, dtype=jnp.int32) * 4 + y_at) * TOK).astype(F32)
    outer = jnp.broadcast_to(starts[:, None, None] * frequencies[None, :, None], (8, HALF, HEAD))
    factor = SCALE * LOG2E
    tables = (jnp.cos(inner) * factor, jnp.sin(inner) * factor, jnp.cos(outer), jnp.sin(outer))
    keys, values = merge(place, blocks, tables)
    received = []
    for step in (2, 1, 3):
        received.append(shift(attend(step, place, keys, values, asked[step]), "y", step))
    return combine([attend(0, place, keys, values, queries), *received])


def solution(mesh):
    split = Mesh(mesh.devices.reshape(4, 2, 4, 4, 2), ("zh", "zl", "y", "x", "core"))
    seq = ("zh", "zl", "y")
    in_specs = (
        P(seq, None),
        P(),
        P(),
        P(None, TP),
        P(TP, None),
        P(None, TP),
        P(seq, TP),
        P(seq),
        P(TP),
        P(None, TP),
        P(seq, TP),
    )
    return jax.shard_map(
        body, mesh=split, in_specs=in_specs, out_specs=P(seq, TP), check_vma=False
    )
```

profile of v0, /device:TPU:224, one launch (start us, length us, event | category | flops | bytes accessed | tf_op | source)
XLA Modules:
  0.0 101.2 jit_solution(4355645470744579009)
XLA Ops:
  2.5 3.1 %convolution_convert_fusion = bf16[128,1280]{1,0:T(8,128)(2,1)S(1)} fusion(bf16[640,1280]{1,0:T(8,128)(2,1)S(1)} %copy-done, bf16[1280,640]{1,0:T(8,128)(2,1)} %param.14, bf16[128,1280]{1,0:T(8,128)(2,1)} %param.11, f32[1280]{0:T(1024)} %param.13, f32[1280]{0:T(1024)} %param.12, f32[128]{0:T(128)S(1)} %add_rsqrt_fusion, f32[128]{0:T(128)S(1)} %broadcast_multiply_fusion), kind=kOutput, calls=%fused_computation | convolution fusion | flops 425902080 | bytes 3943424 | tf_op jit(solution)/shard_map/dot_general | solution.py:362
  7.1 3.1 %collective-permute-start.1 = (bf16[64,1280]{1,0:T(8,128)(2,1)S(1)}, bf16[64,1280]{1,0:T(8,128)(2,1)}, u32[]{:S(2)}, u32[]{:S(2)}) collective-permute-start(bf16[64,1280]{1,0:T(8,128)(2,1)S(1)} %fusion.27), channel_id=1, source_target_pairs={{0,4},{2,6},{4,0},{6,2},{1,5},{3,7},{5,1},{7,3},{8,12},{10,14},{12... | collective-permute-start | bytes 491528 | tf_op jit(solution)/shard_map/ppermute | solution.py:35
  10.8 2.6 %collective-permute-start.3 = (bf16[64,1280]{1,0:T(8,128)(2,1)S(1)}, bf16[64,1280]{1,0:T(8,128)(2,1)}, u32[]{:S(2)}, u32[]{:S(2)}) collective-permute-start(bf16[64,1280]{1,0:T(8,128)(2,1)S(1)} %fusion.27), channel_id=1, source_target_pairs={{0,6},{2,0},{4,2},{6,4},{1,7},{3,1},{5,3},{7,5},{8,14},{10,8},{12,... | collective-permute-start | bytes 491528 | tf_op jit(solution)/shard_map/ppermute | solution.py:35
  13.5 2.2 %copy-done.1 = bf16[2048,1024]{1,0:T(8,128)(2,1)S(1)} copy-done((bf16[2048,1024]{1,0:T(8,128)(2,1)S(1)}, bf16[2048,1024]{1,0:T(8,128)(2,1)}, u32[]{:S(2)}) %copy-start.1) | copy-done | bytes 4194328
  15.7 3.0 %project.2 = (bf16[4,272,256]{2,1,0:T(8,128)(2,1)}, bf16[4,272,256]{2,1,0:T(8,128)(2,1)S(1)}) custom-call(s32[1]{0:T(128)} %bitcast.2.core, bf16[256,1024]{1,0:T(8,128)(2,1)S(1)} %copy-done.4, f32[1,1024]{1,0:T(1,128)S(1)} %bitcast.18, bf16[2048,1024]{1,0:T(8,128)(2,1)S(1)} %copy-done.1), custom_call_target="tpu_custom_call" | custom-call | tf_op jit(solution)/shard_map/project/pallas_call | solution.py:91
  25.6 2.2 %copy-done.2 = bf16[2048,1024]{1,0:T(8,128)(2,1)S(1)} copy-done((bf16[2048,1024]{1,0:T(8,128)(2,1)S(1)}, bf16[2048,1024]{1,0:T(8,128)(2,1)}, u32[]{:S(2)}) %copy-start.2) | copy-done | bytes 4194328
  29.6 2.4 %project.3 = (bf16[4,272,128]{2,1,0:T(8,128)(2,1)S(1)}, bf16[4,272,128]{2,1,0:T(8,128)(2,1)S(1)}) custom-call(s32[1]{0:T(128)} %bitcast.2.core, bf16[64,1280]{1,0:T(8,128)(2,1)S(1)} %fusion.11.half_ref, bf16[64,1280]{1,0:T(8,128)(2,1)S(1)} %collective-permute-done.5.other_ref, bf16[1280,1024]{1,0:T(8,128)(2,1)S(1)} %copy-done.3, f32[1,1024]{1,0:T(1,128)S(1)} %bitcast.19, ...), custom_call_target="tpu_custom_call" | custom-call | tf_op jit(solution)/shard_map/project/pallas_call | solution.py:91
  36.1 2.1 %collective-permute-start.12 = (bf16[272,128]{1,0:T(8,128)(2,1)S(1)}, bf16[272,128]{1,0:T(8,128)(2,1)S(1)}, u32[]{:S(2)}, u32[]{:S(2)}) collective-permute-start(bf16[272,128]{1,0:T(8,128)(2,1)S(1)} %get-tuple-element.56), channel_id=1, source_target_pairs={{0,6},{2,0},{4,2},{6,4},{1,7},{3,1},{5,3},{7,5},{8,14},{10,8},{12,... | collective-permute-start | bytes 208904 | tf_op jit(solution)/shard_map/ppermute | solution.py:35
  41.4 2.1 %collective-permute-start.21 = (bf16[256,512]{1,0:T(8,128)(2,1)S(1)}, bf16[256,512]{1,0:T(8,128)(2,1)}, u32[]{:S(2)}, u32[]{:S(2)}) collective-permute-start(bf16[256,512]{1,0:T(8,128)(2,1)S(1)} %copy-done.7), channel_id=1, source_target_pairs={{0,16},{8,24},{16,0},{24,8},{1,17},{9,25},{17,1},{25,9},{2,18},{10... | collective-permute-start | bytes 786440 | tf_op jit(solution)/shard_map/ppermute | solution.py:35
  45.3 2.2 %collective-permute-start.13 = (bf16[272,384]{1,0:T(8,128)(2,1)S(1)}, bf16[272,384]{1,0:T(8,128)(2,1)S(1)}, u32[]{:S(2)}, u32[]{:S(2)}) collective-permute-start(bf16[272,384]{1,0:T(8,128)(2,1)S(1)} %finish_rows.1.refs_0_), channel_id=1, source_target_pairs={{0,32},{32,64},{64,96},{96,128},{128,160},{160,192},{192,224},{224... | collective-permute-start | bytes 626696 | tf_op jit(solution)/shard_map/ppermute | solution.py:35
  47.5 3.8 %collective-permute-done.14.refs_2_ = bf16[272,384]{1,0:T(8,128)(2,1)S(1)} collective-permute-done((bf16[272,384]{1,0:T(8,128)(2,1)S(1)}, bf16[272,384]{1,0:T(8,128)(2,1)S(1)}, u32[]{:S(2)}, u32[]{:S(2)}) %collective-permute-start.14) | collective-permute-done | bytes 208928 | tf_op jit(solution)/shard_map/ppermute | solution.py:35
  51.3 3.2 %collective-permute-start.15 = (bf16[272,384]{1,0:T(8,128)(2,1)S(1)}, bf16[272,384]{1,0:T(8,128)(2,1)S(1)}, u32[]{:S(2)}, u32[]{:S(2)}) collective-permute-start(bf16[272,384]{1,0:T(8,128)(2,1)S(1)} %collective-permute-done.13.refs_1_), channel_id=1, source_target_pairs={{0,32},{32,64},{64,96},{96,128},{128,160},{160,192},{192,224},{224... | collective-permute-start | bytes 626696 | tf_op jit(solution)/shard_map/ppermute | solution.py:35
  54.8 3.5 %collective-permute-done.16.refs_4_ = bf16[272,384]{1,0:T(8,128)(2,1)S(1)} collective-permute-done((bf16[272,384]{1,0:T(8,128)(2,1)S(1)}, bf16[272,384]{1,0:T(8,128)(2,1)S(1)}, u32[]{:S(2)}, u32[]{:S(2)}) %collective-permute-start.16) | collective-permute-done | bytes 208928 | tf_op jit(solution)/shard_map/ppermute | solution.py:35
  58.4 3.5 %collective-permute-start.17 = (bf16[272,384]{1,0:T(8,128)(2,1)S(1)}, bf16[272,384]{1,0:T(8,128)(2,1)S(1)}, u32[]{:S(2)}, u32[]{:S(2)}) collective-permute-start(bf16[272,384]{1,0:T(8,128)(2,1)S(1)} %collective-permute-done.15.refs_3_), channel_id=1, source_target_pairs={{0,32},{32,64},{64,96},{96,128},{128,160},{160,192},{192,224},{224... | collective-permute-start | bytes 626696 | tf_op jit(solution)/shard_map/ppermute | solution.py:35
  62.0 4.5 %collective-permute-done.18.refs_6_ = bf16[272,384]{1,0:T(8,128)(2,1)S(1)} collective-permute-done((bf16[272,384]{1,0:T(8,128)(2,1)S(1)}, bf16[272,384]{1,0:T(8,128)(2,1)S(1)}, u32[]{:S(2)}, u32[]{:S(2)}) %collective-permute-start.18) | collective-permute-done | bytes 208928 | tf_op jit(solution)/shard_map/ppermute | solution.py:35
  66.6 3.4 %collective-permute-start.19 = (bf16[128,384]{1,0:T(8,128)(2,1)S(1)}, bf16[128,384]{1,0:T(8,128)(2,1)S(1)}, u32[]{:S(2)}, u32[]{:S(2)}) collective-permute-start(bf16[128,384]{1,0:T(8,128)(2,1)S(1)} %slice.8), channel_id=1, source_target_pairs={{0,32},{32,64},{64,96},{96,128},{128,160},{160,192},{192,224},{224... | collective-permute-start | bytes 294920 | tf_op jit(solution)/shard_map/ppermute | solution.py:35
  70.1 2.1 %collective-permute-done.19.refs_7_ = bf16[128,384]{1,0:T(8,128)(2,1)S(1)} collective-permute-done((bf16[128,384]{1,0:T(8,128)(2,1)S(1)}, bf16[128,384]{1,0:T(8,128)(2,1)S(1)}, u32[]{:S(2)}, u32[]{:S(2)}) %collective-permute-start.19) | collective-permute-done | bytes 98336 | tf_op jit(solution)/shard_map/ppermute | solution.py:35
  72.8 1.8 %merge.1 = (bf16[128,2048]{1,0:T(8,128)(2,1)S(1)}, bf16[2048,256]{1,0:T(8,128)(2,1)S(1)}) custom-call(s32[2]{0:T(128)S(1)} %pad_add_fusion.place, bf16[272,384]{1,0:T(8,128)(2,1)S(1)} %finish_rows.1.refs_0_, bf16[272,384]{1,0:T(8,128)(2,1)S(1)} %collective-permute-done.13.refs_1_, bf16[272,384]{1,0:T(8,128)(2,1)S(1)} %collective-permute-done.14.refs_2_, ...), custom_call_target="tpu_custom_call" | custom-call | tf_op jit(solution)/shard_map/merge/pallas_call | solution.py:194
  74.6 4.8 %attend.7 = bf16[272,512]{1,0:T(8,128)(2,1)S(1)} custom-call(s32[2]{0:T(128)S(1)} %pad_add_fusion.place, bf16[128,2048]{1,0:T(8,128)(2,1)S(1)} %get-tuple-element.57.keys, bf16[2048,256]{1,0:T(8,128)(2,1)S(1)} %get-tuple-element.58.values, bf16[256,512]{1,0:T(8,128)(2,1)} %collective-permute-done.25.query_ref), custom_call_target="tpu_custom_call" | custom-call | flops 1073741824 | bytes 2097152 | tf_op jit(solution)/shard_map/attend/pallas_call | solution.py:280
  79.8 5.0 %attend.6 = bf16[272,512]{1,0:T(8,128)(2,1)S(1)} custom-call(s32[2]{0:T(128)S(1)} %pad_add_fusion.place, bf16[128,2048]{1,0:T(8,128)(2,1)S(1)} %get-tuple-element.57.keys, bf16[2048,256]{1,0:T(8,128)(2,1)S(1)} %get-tuple-element.58.values, bf16[256,512]{1,0:T(8,128)(2,1)} %collective-permute-done.23.query_ref), custom_call_target="tpu_custom_call" | custom-call | flops 1073741824 | bytes 2097152 | tf_op jit(solution)/shard_map/attend/pallas_call | solution.py:280
  84.9 1.8 %collective-permute-start.24 = (bf16[272,512]{1,0:T(8,128)(2,1)S(1)}, bf16[272,512]{1,0:T(8,128)(2,1)S(1)}, u32[]{:S(2)}, u32[]{:S(2)}) collective-permute-start(bf16[272,512]{1,0:T(8,128)(2,1)S(1)} %attend.6), channel_id=1, source_target_pairs={{0,8},{8,16},{16,24},{24,0},{1,9},{9,17},{17,25},{25,1},{2,10},{10... | collective-permute-start | bytes 835592 | tf_op jit(solution)/shard_map/ppermute | solution.py:35
  86.7 4.8 %attend.5 = bf16[272,512]{1,0:T(8,128)(2,1)S(1)} custom-call(s32[2]{0:T(128)S(1)} %pad_add_fusion.place, bf16[128,2048]{1,0:T(8,128)(2,1)S(1)} %get-tuple-element.57.keys, bf16[2048,256]{1,0:T(8,128)(2,1)S(1)} %get-tuple-element.58.values, bf16[256,512]{1,0:T(8,128)(2,1)} %collective-permute-done.21.query_ref), custom_call_target="tpu_custom_call" | custom-call | flops 1073741824 | bytes 2097152 | tf_op jit(solution)/shard_map/attend/pallas_call | solution.py:280
  92.4 4.4 %attend.4.refs_0_ = bf16[272,512]{1,0:T(8,128)(2,1)S(1)} custom-call(s32[2]{0:T(128)S(1)} %pad_add_fusion.place, bf16[128,2048]{1,0:T(8,128)(2,1)S(1)} %get-tuple-element.57.keys, bf16[2048,256]{1,0:T(8,128)(2,1)S(1)} %get-tuple-element.58.values, bf16[256,512]{1,0:T(8,128)(2,1)S(1)} %copy-done.7), custom_call_target="tpu_custom_call" | custom-call | flops 1073741824 | bytes 2097152 | tf_op jit(solution)/shard_map/attend/pallas_call | solution.py:280
  96.9 2.8 %collective-permute-done.22.refs_1_ = bf16[272,512]{1,0:T(8,128)(2,1)S(1)} collective-permute-done((bf16[272,512]{1,0:T(8,128)(2,1)S(1)}, bf16[272,512]{1,0:T(8,128)(2,1)S(1)}, u32[]{:S(2)}, u32[]{:S(2)}) %collective-permute-start.22) | collective-permute-done | bytes 278560 | tf_op jit(solution)/shard_map/ppermute | solution.py:35
  (78 shorter events, 26.2 us)
Async XLA Ops:
  7.1 11.5 %collective-permute-start.1 = (bf16[64,1280]{1,0:T(8,128)(2,1)S(1)}, bf16[64,1280]{1,0:T(8,128)(2,1)}, u32[]{:S(2)}, u32[]{:S(2)}) collective-permute-start(bf16[64,1280]{1,0:T(8,128)(2,1)S(1)} %fusion.27), channel_id=1, source_target_pairs={{0,4},{2,6},{4,0},{6,2},{1,5},{3,7},{5,1},{7,3},{8,12},{10,14},{12... | collective-permute-start | bytes 491528 | tf_op jit(solution)/shard_map/ppermute | solution.py:35
  10.3 8.4 %collective-permute-start.2 = (bf16[64,1280]{1,0:T(8,128)(2,1)S(1)}, bf16[64,1280]{1,0:T(8,128)(2,1)}, u32[]{:S(2)}, u32[]{:S(2)}) collective-permute-start(bf16[64,1280]{1,0:T(8,128)(2,1)S(1)} %fusion.27), channel_id=1, source_target_pairs={{0,2},{2,4},{4,6},{6,0},{1,3},{3,5},{5,7},{7,1},{8,10},{10,12},{12... | collective-permute-start | bytes 491528 | tf_op jit(solution)/shard_map/ppermute | solution.py:35
  10.8 7.8 %collective-permute-start.3 = (bf16[64,1280]{1,0:T(8,128)(2,1)S(1)}, bf16[64,1280]{1,0:T(8,128)(2,1)}, u32[]{:S(2)}, u32[]{:S(2)}) collective-permute-start(bf16[64,1280]{1,0:T(8,128)(2,1)S(1)} %fusion.27), channel_id=1, source_target_pairs={{0,6},{2,0},{4,2},{6,4},{1,7},{3,1},{5,3},{7,5},{8,14},{10,8},{12,... | collective-permute-start | bytes 491528 | tf_op jit(solution)/shard_map/ppermute | solution.py:35
  21.0 4.7 %collective-permute-start.5 = (bf16[64,1280]{1,0:T(8,128)(2,1)S(1)}, bf16[64,1280]{1,0:T(8,128)(2,1)S(1)}, u32[]{:S(2)}, u32[]{:S(2)}) collective-permute-start(bf16[64,1280]{1,0:T(8,128)(2,1)S(1)} %fusion.11.half_ref), channel_id=1, source_target_pairs={{0,1},{1,0},{2,3},{3,2},{4,5},{5,4},{6,7},{7,6},{8,9},{9,8},{10,11... | collective-permute-start | bytes 491528 | tf_op jit(solution)/shard_map/ppermute | solution.py:35
  21.2 10.8 %collective-permute-start.6 = (bf16[272,256]{1,0:T(8,128)(2,1)S(1)}, bf16[272,256]{1,0:T(8,128)(2,1)S(1)}, u32[]{:S(2)}, u32[]{:S(2)}) collective-permute-start(bf16[272,256]{1,0:T(8,128)(2,1)S(1)} %get-tuple-element.44), channel_id=1, source_target_pairs={{0,4},{2,6},{4,0},{6,2},{1,5},{3,7},{5,1},{7,3},{8,12},{10,14},{12... | collective-permute-start | bytes 417800 | tf_op jit(solution)/shard_map/ppermute | solution.py:35
  22.4 9.6 %collective-permute-start.7 = (bf16[272,256]{1,0:T(8,128)(2,1)S(1)}, bf16[272,256]{1,0:T(8,128)(2,1)S(1)}, u32[]{:S(2)}, u32[]{:S(2)}) collective-permute-start(bf16[272,256]{1,0:T(8,128)(2,1)S(1)} %get-tuple-element.45), channel_id=1, source_target_pairs={{0,2},{2,4},{4,6},{6,0},{1,3},{3,5},{5,7},{7,1},{8,10},{10,12},{12... | collective-permute-start | bytes 417800 | tf_op jit(solution)/shard_map/ppermute | solution.py:35
  23.9 8.2 %collective-permute-start.8 = (bf16[272,256]{1,0:T(8,128)(2,1)S(1)}, bf16[272,256]{1,0:T(8,128)(2,1)S(1)}, u32[]{:S(2)}, u32[]{:S(2)}) collective-permute-start(bf16[272,256]{1,0:T(8,128)(2,1)S(1)} %get-tuple-element.46), channel_id=1, source_target_pairs={{0,6},{2,0},{4,2},{6,4},{1,7},{3,1},{5,3},{7,5},{8,14},{10,8},{12,... | collective-permute-start | bytes 417800 | tf_op jit(solution)/shard_map/ppermute | solution.py:35
  33.7 7.7 %collective-permute-start.10 = (bf16[272,128]{1,0:T(8,128)(2,1)S(1)}, bf16[272,128]{1,0:T(8,128)(2,1)S(1)}, u32[]{:S(2)}, u32[]{:S(2)}) collective-permute-start(bf16[272,128]{1,0:T(8,128)(2,1)S(1)} %get-tuple-element.54), channel_id=1, source_target_pairs={{0,4},{2,6},{4,0},{6,2},{1,5},{3,7},{5,1},{7,3},{8,12},{10,14},{12... | collective-permute-start | bytes 208904 | tf_op jit(solution)/shard_map/ppermute | solution.py:35
  34.9 8.6 %collective-permute-start.11 = (bf16[272,128]{1,0:T(8,128)(2,1)S(1)}, bf16[272,128]{1,0:T(8,128)(2,1)S(1)}, u32[]{:S(2)}, u32[]{:S(2)}) collective-permute-start(bf16[272,128]{1,0:T(8,128)(2,1)S(1)} %get-tuple-element.55), channel_id=1, source_target_pairs={{0,2},{2,4},{4,6},{6,0},{1,3},{3,5},{5,7},{7,1},{8,10},{10,12},{12... | collective-permute-start | bytes 208904 | tf_op jit(solution)/shard_map/ppermute | solution.py:35
  36.1 7.5 %collective-permute-start.12 = (bf16[272,128]{1,0:T(8,128)(2,1)S(1)}, bf16[272,128]{1,0:T(8,128)(2,1)S(1)}, u32[]{:S(2)}, u32[]{:S(2)}) collective-permute-start(bf16[272,128]{1,0:T(8,128)(2,1)S(1)} %get-tuple-element.56), channel_id=1, source_target_pairs={{0,6},{2,0},{4,2},{6,4},{1,7},{3,1},{5,3},{7,5},{8,14},{10,8},{12,... | collective-permute-start | bytes 208904 | tf_op jit(solution)/shard_map/ppermute | solution.py:35
  38.2 36.4 %collective-permute-start.25 = (bf16[256,512]{1,0:T(8,128)(2,1)S(1)}, bf16[256,512]{1,0:T(8,128)(2,1)}, u32[]{:S(2)}, u32[]{:S(2)}) collective-permute-start(bf16[256,512]{1,0:T(8,128)(2,1)S(1)} %copy-done.7), channel_id=1, source_target_pairs={{0,8},{8,16},{16,24},{24,0},{1,9},{9,17},{17,25},{25,1},{2,10},{10... | collective-permute-start | bytes 786440 | tf_op jit(solution)/shard_map/ppermute | solution.py:35
  39.8 40.0 %collective-permute-start.23 = (bf16[256,512]{1,0:T(8,128)(2,1)S(1)}, bf16[256,512]{1,0:T(8,128)(2,1)}, u32[]{:S(2)}, u32[]{:S(2)}) collective-permute-start(bf16[256,512]{1,0:T(8,128)(2,1)S(1)} %copy-done.7), channel_id=1, source_target_pairs={{0,24},{8,0},{16,8},{24,16},{1,25},{9,1},{17,9},{25,17},{2,26},{10... | collective-permute-start | bytes 786440 | tf_op jit(solution)/shard_map/ppermute | solution.py:35
  41.4 45.3 %collective-permute-start.21 = (bf16[256,512]{1,0:T(8,128)(2,1)S(1)}, bf16[256,512]{1,0:T(8,128)(2,1)}, u32[]{:S(2)}, u32[]{:S(2)}) collective-permute-start(bf16[256,512]{1,0:T(8,128)(2,1)S(1)} %copy-done.7), channel_id=1, source_target_pairs={{0,16},{8,24},{16,0},{24,8},{1,17},{9,25},{17,1},{25,9},{2,18},{10... | collective-permute-start | bytes 786440 | tf_op jit(solution)/shard_map/ppermute | solution.py:35
  44.2 7.1 %collective-permute-start.14 = (bf16[272,384]{1,0:T(8,128)(2,1)S(1)}, bf16[272,384]{1,0:T(8,128)(2,1)S(1)}, u32[]{:S(2)}, u32[]{:S(2)}) collective-permute-start(bf16[272,384]{1,0:T(8,128)(2,1)S(1)} %finish_rows.1.refs_0_), channel_id=1, source_target_pairs={{0,224},{32,0},{64,32},{96,64},{128,96},{160,128},{192,160},{224,1... | collective-permute-start | bytes 626696 | tf_op jit(solution)/shard_map/ppermute | solution.py:35
  45.3 6.0 %collective-permute-start.13 = (bf16[272,384]{1,0:T(8,128)(2,1)S(1)}, bf16[272,384]{1,0:T(8,128)(2,1)S(1)}, u32[]{:S(2)}, u32[]{:S(2)}) collective-permute-start(bf16[272,384]{1,0:T(8,128)(2,1)S(1)} %finish_rows.1.refs_0_), channel_id=1, source_target_pairs={{0,32},{32,64},{64,96},{96,128},{128,160},{160,192},{192,224},{224... | collective-permute-start | bytes 626696 | tf_op jit(solution)/shard_map/ppermute | solution.py:35
  51.3 7.1 %collective-permute-start.16 = (bf16[272,384]{1,0:T(8,128)(2,1)S(1)}, bf16[272,384]{1,0:T(8,128)(2,1)S(1)}, u32[]{:S(2)}, u32[]{:S(2)}) collective-permute-start(bf16[272,384]{1,0:T(8,128)(2,1)S(1)} %collective-permute-done.14.refs_2_), channel_id=1, source_target_pairs={{0,224},{32,0},{64,32},{96,64},{128,96},{160,128},{192,160},{224,1... | collective-permute-start | bytes 626696 | tf_op jit(solution)/shard_map/ppermute | solution.py:35
  51.3 7.1 %collective-permute-start.15 = (bf16[272,384]{1,0:T(8,128)(2,1)S(1)}, bf16[272,384]{1,0:T(8,128)(2,1)S(1)}, u32[]{:S(2)}, u32[]{:S(2)}) collective-permute-start(bf16[272,384]{1,0:T(8,128)(2,1)S(1)} %collective-permute-done.13.refs_1_), channel_id=1, source_target_pairs={{0,32},{32,64},{64,96},{96,128},{128,160},{160,192},{192,224},{224... | collective-permute-start | bytes 626696 | tf_op jit(solution)/shard_map/ppermute | solution.py:35
  58.3 8.1 %collective-permute-start.18 = (bf16[272,384]{1,0:T(8,128)(2,1)S(1)}, bf16[272,384]{1,0:T(8,128)(2,1)S(1)}, u32[]{:S(2)}, u32[]{:S(2)}) collective-permute-start(bf16[272,384]{1,0:T(8,128)(2,1)S(1)} %collective-permute-done.16.refs_4_), channel_id=1, source_target_pairs={{0,224},{32,0},{64,32},{96,64},{128,96},{160,128},{192,160},{224,1... | collective-permute-start | bytes 626696 | tf_op jit(solution)/shard_map/ppermute | solution.py:35
  58.4 8.2 %collective-permute-start.17 = (bf16[272,384]{1,0:T(8,128)(2,1)S(1)}, bf16[272,384]{1,0:T(8,128)(2,1)S(1)}, u32[]{:S(2)}, u32[]{:S(2)}) collective-permute-start(bf16[272,384]{1,0:T(8,128)(2,1)S(1)} %collective-permute-done.15.refs_3_), channel_id=1, source_target_pairs={{0,32},{32,64},{64,96},{96,128},{128,160},{160,192},{192,224},{224... | collective-permute-start | bytes 626696 | tf_op jit(solution)/shard_map/ppermute | solution.py:35
  66.5 6.0 %collective-permute-start.20 = (bf16[144,384]{1,0:T(8,128)(2,1)S(1)}, bf16[144,384]{1,0:T(8,128)(2,1)S(1)}, u32[]{:S(2)}, u32[]{:S(2)}) collective-permute-start(bf16[144,384]{1,0:T(8,128)(2,1)S(1)} %slice.9), channel_id=1, source_target_pairs={{0,224},{32,0},{64,32},{96,64},{128,96},{160,128},{192,160},{224,1... | collective-permute-start | bytes 331784 | tf_op jit(solution)/shard_map/ppermute | solution.py:35
  66.6 5.6 %collective-permute-start.19 = (bf16[128,384]{1,0:T(8,128)(2,1)S(1)}, bf16[128,384]{1,0:T(8,128)(2,1)S(1)}, u32[]{:S(2)}, u32[]{:S(2)}) collective-permute-start(bf16[128,384]{1,0:T(8,128)(2,1)S(1)} %slice.8), channel_id=1, source_target_pairs={{0,32},{32,64},{64,96},{96,128},{128,160},{160,192},{192,224},{224... | collective-permute-start | bytes 294920 | tf_op jit(solution)/shard_map/ppermute | solution.py:35
  79.4 17.5 %collective-permute-start.26 = (bf16[272,512]{1,0:T(8,128)(2,1)S(1)}, bf16[272,512]{1,0:T(8,128)(2,1)S(1)}, u32[]{:S(2)}, u32[]{:S(2)}) collective-permute-start(bf16[272,512]{1,0:T(8,128)(2,1)S(1)} %attend.7), channel_id=1, source_target_pairs={{0,24},{8,0},{16,8},{24,16},{1,25},{9,1},{17,9},{25,17},{2,26},{10... | collective-permute-start | bytes 835592 | tf_op jit(solution)/shard_map/ppermute | solution.py:35
  84.9 12.0 %collective-permute-start.24 = (bf16[272,512]{1,0:T(8,128)(2,1)S(1)}, bf16[272,512]{1,0:T(8,128)(2,1)S(1)}, u32[]{:S(2)}, u32[]{:S(2)}) collective-permute-start(bf16[272,512]{1,0:T(8,128)(2,1)S(1)} %attend.6), channel_id=1, source_target_pairs={{0,8},{8,16},{16,24},{24,0},{1,9},{9,17},{17,25},{25,1},{2,10},{10... | collective-permute-start | bytes 835592 | tf_op jit(solution)/shard_map/ppermute | solution.py:35
  91.5 8.1 %collective-permute-start.22 = (bf16[272,512]{1,0:T(8,128)(2,1)S(1)}, bf16[272,512]{1,0:T(8,128)(2,1)S(1)}, u32[]{:S(2)}, u32[]{:S(2)}) collective-permute-start(bf16[272,512]{1,0:T(8,128)(2,1)S(1)} %attend.5), channel_id=1, source_target_pairs={{0,16},{8,24},{16,0},{24,8},{1,17},{9,25},{17,1},{25,9},{2,18},{10... | collective-permute-start | bytes 835592 | tf_op jit(solution)/shard_map/ppermute | solution.py:35
  (13 other events, 78.0 us)
where the time goes:
time: 102 us; the launch traced here: 101 us
  starting transfers between devices  37.6 us (37%)
  Pallas kernels  28.7 us (28%)
  waiting for transfers between devices  20.7 us (20%)
  local copies, waits for them, and re-layouts  6.44 us (6%)
  other arithmetic  4.29 us (4%)
  matrix products  3.08 us (3%)
    ppermute x27, starting transfers between devices, shift(): lax.ppermute(values, axis, [(i, (i + step) % count) for i in range(count)])  37.6 us
    ppermute x27, waiting for transfers between devices, shift(): lax.ppermute(values, axis, [(i, (i + step) % count) for i in range(count)])  20.7 us
    pallas_call x4, Pallas kernels, attend(): pl.pallas_call(functools.partial(attend_kernel, step), out_shape=jax.Shap...  19.2 us
    unnamed x20, local copies, waits for them, and re-layouts  6.15 us
    pallas_call x2, Pallas kernels, project(): pl.pallas_call(kernel, out_shape=(shape, shape), in_specs=[pl.BlockSpec(m...  5.38 us
    dot_general x1, matrix products, body(): jnp.dot(enc_hidden, encoder_down, preferred_element_type=F32).astype(BF16)  3.08 us
  transfers between devices with their start and end apart: 27, of which 9 were waited for; matrix products, arithmetic and copies ran while one was open for 2% of the time, Pallas kernels for 27%

commit v1 on v0

--- a/solution.py
+++ b/solution.py
@@ -51,8 +51,7 @@
 
 
 def head_rows(core, features, tail, weight_ref, give_ref, keep_ref):
-    @pl.loop(0, 4)
-    def one_chip(x_at):
+    for x_at in range(4):
         for own, ref in ((0, give_ref), (1, keep_ref)):
             head = 2 * x_at + jnp.where(own == 1, core, 1 - core)
             weight = weight_ref[pl.ds(pl.multiple_of(head * TOK, TOK), TOK), :]

time: 102 us -> 101 us (level)
  starting transfers between devices: 37.6 us -> 39.8 us
  Pallas kernels: 28.7 us -> 26.9 us
    ppermute x27, starting transfers between devices: 37.6 us -> 39.8 us  [shift(): lax.ppermute(values, axis, [(i, (i + step) % count) for i in range(count)])]
    pallas_call x2, Pallas kernels: 5.38 us -> 3.77 us  [project(): pl.pallas_call(kernel, out_shape=(shape, shape), in_specs=[pl.BlockSpec(m...]
  transfers between devices with their start and end apart: 27 -> 27, of which waited for: 9 -> 10; matrix products, arithmetic and copies ran while one was open for 2% -> 2% of each run, Pallas kernels for 27% -> 25%
where the time goes in v1:
time: 101 us
  starting transfers between devices  39.8 us (39%)
  Pallas kernels  26.9 us (27%)
  waiting for transfers between devices  19.9 us (20%)
  local copies, waits for them, and re-layouts  6.44 us (6%)
  other arithmetic  4.29 us (4%)
  matrix products  3.08 us (3%)
    ppermute x27, starting transfers between devices, shift(): lax.ppermute(values, axis, [(i, (i + step) % count) for i in range(count)])  39.8 us
    ppermute x27, waiting for transfers between devices, shift(): lax.ppermute(values, axis, [(i, (i + step) % count) for i in range(count)])  19.9 us
    pallas_call x4, Pallas kernels, attend(): pl.pallas_call(functools.partial(attend_kernel, step), out_shape=jax.Shap...  19 us
    unnamed x20, local copies, waits for them, and re-layouts  6.15 us
    pallas_call x2, Pallas kernels, project(): pl.pallas_call(kernel, out_shape=(shape, shape), in_specs=[pl.BlockSpec(m...  3.77 us
    dot_general x1, matrix products, body(): jnp.dot(enc_hidden, encoder_down, preferred_element_type=F32).astype(BF16)  3.08 us
  transfers between devices with their start and end apart: 27, of which 10 were waited for; matrix products, arithmetic and copies ran while one was open for 2% of the time, Pallas kernels for 25%

profile of v1, /device:TPU:224, one launch (start us, length us, event | category | flops | bytes accessed | tf_op | source)
XLA Modules:
  0.0 100.7 jit_solution(9145632048657136961)
XLA Ops:
  2.5 3.1 %convolution_convert_fusion = bf16[128,1280]{1,0:T(8,128)(2,1)S(1)} fusion(bf16[640,1280]{1,0:T(8,128)(2,1)S(1)} %copy-done, bf16[1280,640]{1,0:T(8,128)(2,1)} %param.14, bf16[128,1280]{1,0:T(8,128)(2,1)} %param.11, f32[1280]{0:T(1024)} %param.13, f32[1280]{0:T(1024)} %param.12, f32[128]{0:T(128)S(1)} %add_rsqrt_fusion, f32[128]{0:T(128)S(1)} %broadcast_multiply_fusion), kind=kOutput, calls=%fused_computation | convolution fusion | flops 425902080 | bytes 3943424 | tf_op jit(solution)/shard_map/dot_general | solution.py:361
  7.1 3.1 %collective-permute-start.1 = (bf16[64,1280]{1,0:T(8,128)(2,1)S(1)}, bf16[64,1280]{1,0:T(8,128)(2,1)}, u32[]{:S(2)}, u32[]{:S(2)}) collective-permute-start(bf16[64,1280]{1,0:T(8,128)(2,1)S(1)} %fusion.27), channel_id=1, source_target_pairs={{0,4},{2,6},{4,0},{6,2},{1,5},{3,7},{5,1},{7,3},{8,12},{10,14},{12... | collective-permute-start | bytes 491528 | tf_op jit(solution)/shard_map/ppermute | solution.py:35
  10.8 2.6 %collective-permute-start.3 = (bf16[64,1280]{1,0:T(8,128)(2,1)S(1)}, bf16[64,1280]{1,0:T(8,128)(2,1)}, u32[]{:S(2)}, u32[]{:S(2)}) collective-permute-start(bf16[64,1280]{1,0:T(8,128)(2,1)S(1)} %fusion.27), channel_id=1, source_target_pairs={{0,6},{2,0},{4,2},{6,4},{1,7},{3,1},{5,3},{7,5},{8,14},{10,8},{12,... | collective-permute-start | bytes 491528 | tf_op jit(solution)/shard_map/ppermute | solution.py:35
  13.5 2.2 %copy-done.1 = bf16[2048,1024]{1,0:T(8,128)(2,1)S(1)} copy-done((bf16[2048,1024]{1,0:T(8,128)(2,1)S(1)}, bf16[2048,1024]{1,0:T(8,128)(2,1)}, u32[]{:S(2)}) %copy-start.1) | copy-done | bytes 4194328
  15.7 2.1 %project.2 = (bf16[4,272,256]{2,1,0:T(8,128)(2,1)}, bf16[4,272,256]{2,1,0:T(8,128)(2,1)S(1)}) custom-call(s32[1]{0:T(128)} %bitcast.2.core, bf16[256,1024]{1,0:T(8,128)(2,1)S(1)} %copy-done.4, f32[1,1024]{1,0:T(1,128)S(1)} %bitcast.18, bf16[2048,1024]{1,0:T(8,128)(2,1)S(1)} %copy-done.1), custom_call_target="tpu_custom_call" | custom-call | tf_op jit(solution)/shard_map/project/pallas_call | solution.py:90
  20.4 2.0 %collective-permute-start.6 = (bf16[272,256]{1,0:T(8,128)(2,1)S(1)}, bf16[272,256]{1,0:T(8,128)(2,1)S(1)}, u32[]{:S(2)}, u32[]{:S(2)}) collective-permute-start(bf16[272,256]{1,0:T(8,128)(2,1)S(1)} %get-tuple-element.44), channel_id=1, source_target_pairs={{0,4},{2,6},{4,0},{6,2},{1,5},{3,7},{5,1},{7,3},{8,12},{10,14},{12... | collective-permute-start | bytes 417800 | tf_op jit(solution)/shard_map/ppermute | solution.py:35
  23.9 1.8 %collective-permute-start.8 = (bf16[272,256]{1,0:T(8,128)(2,1)S(1)}, bf16[272,256]{1,0:T(8,128)(2,1)S(1)}, u32[]{:S(2)}, u32[]{:S(2)}) collective-permute-start(bf16[272,256]{1,0:T(8,128)(2,1)S(1)} %get-tuple-element.46), channel_id=1, source_target_pairs={{0,6},{2,0},{4,2},{6,4},{1,7},{3,1},{5,3},{7,5},{8,14},{10,8},{12,... | collective-permute-start | bytes 417800 | tf_op jit(solution)/shard_map/ppermute | solution.py:35
  25.6 2.2 %copy-done.2 = bf16[2048,1024]{1,0:T(8,128)(2,1)S(1)} copy-done((bf16[2048,1024]{1,0:T(8,128)(2,1)S(1)}, bf16[2048,1024]{1,0:T(8,128)(2,1)}, u32[]{:S(2)}) %copy-start.2) | copy-done | bytes 4194328
  36.1 1.8 %collective-permute-start.12 = (bf16[272,128]{1,0:T(8,128)(2,1)S(1)}, bf16[272,128]{1,0:T(8,128)(2,1)S(1)}, u32[]{:S(2)}, u32[]{:S(2)}) collective-permute-start(bf16[272,128]{1,0:T(8,128)(2,1)S(1)} %get-tuple-element.56), channel_id=1, source_target_pairs={{0,6},{2,0},{4,2},{6,4},{1,7},{3,1},{5,3},{7,5},{8,14},{10,8},{12,... | collective-permute-start | bytes 208904 | tf_op jit(solution)/shard_map/ppermute | solution.py:35
  41.1 2.0 %collective-permute-start.21 = (bf16[256,512]{1,0:T(8,128)(2,1)S(1)}, bf16[256,512]{1,0:T(8,128)(2,1)}, u32[]{:S(2)}, u32[]{:S(2)}) collective-permute-start(bf16[256,512]{1,0:T(8,128)(2,1)S(1)} %copy-done.7), channel_id=1, source_target_pairs={{0,16},{8,24},{16,0},{24,8},{1,17},{9,25},{17,1},{25,9},{2,18},{10... | collective-permute-start | bytes 786440 | tf_op jit(solution)/shard_map/ppermute | solution.py:35
  44.9 2.2 %collective-permute-start.13 = (bf16[272,384]{1,0:T(8,128)(2,1)S(1)}, bf16[272,384]{1,0:T(8,128)(2,1)S(1)}, u32[]{:S(2)}, u32[]{:S(2)}) collective-permute-start(bf16[272,384]{1,0:T(8,128)(2,1)S(1)} %finish_rows.1.refs_0_), channel_id=1, source_target_pairs={{0,32},{32,64},{64,96},{96,128},{128,160},{160,192},{192,224},{224... | collective-permute-start | bytes 626696 | tf_op jit(solution)/shard_map/ppermute | solution.py:35
  47.1 3.8 %collective-permute-done.14.refs_2_ = bf16[272,384]{1,0:T(8,128)(2,1)S(1)} collective-permute-done((bf16[272,384]{1,0:T(8,128)(2,1)S(1)}, bf16[272,384]{1,0:T(8,128)(2,1)S(1)}, u32[]{:S(2)}, u32[]{:S(2)}) %collective-permute-start.14) | collective-permute-done | bytes 208928 | tf_op jit(solution)/shard_map/ppermute | solution.py:35
  50.9 3.2 %collective-permute-start.15 = (bf16[272,384]{1,0:T(8,128)(2,1)S(1)}, bf16[272,384]{1,0:T(8,128)(2,1)S(1)}, u32[]{:S(2)}, u32[]{:S(2)}) collective-permute-start(bf16[272,384]{1,0:T(8,128)(2,1)S(1)} %collective-permute-done.13.refs_1_), channel_id=1, source_target_pairs={{0,32},{32,64},{64,96},{96,128},{128,160},{160,192},{192,224},{224... | collective-permute-start | bytes 626696 | tf_op jit(solution)/shard_map/ppermute | solution.py:35
  54.5 3.5 %collective-permute-done.16.refs_4_ = bf16[272,384]{1,0:T(8,128)(2,1)S(1)} collective-permute-done((bf16[272,384]{1,0:T(8,128)(2,1)S(1)}, bf16[272,384]{1,0:T(8,128)(2,1)S(1)}, u32[]{:S(2)}, u32[]{:S(2)}) %collective-permute-start.16) | collective-permute-done | bytes 208928 | tf_op jit(solution)/shard_map/ppermute | solution.py:35
  57.9 3.5 %collective-permute-start.17 = (bf16[272,384]{1,0:T(8,128)(2,1)S(1)}, bf16[272,384]{1,0:T(8,128)(2,1)S(1)}, u32[]{:S(2)}, u32[]{:S(2)}) collective-permute-start(bf16[272,384]{1,0:T(8,128)(2,1)S(1)} %collective-permute-done.15.refs_3_), channel_id=1, source_target_pairs={{0,32},{32,64},{64,96},{96,128},{128,160},{160,192},{192,224},{224... | collective-permute-start | bytes 626696 | tf_op jit(solution)/shard_map/ppermute | solution.py:35
  61.5 4.4 %collective-permute-done.18.refs_6_ = bf16[272,384]{1,0:T(8,128)(2,1)S(1)} collective-permute-done((bf16[272,384]{1,0:T(8,128)(2,1)S(1)}, bf16[272,384]{1,0:T(8,128)(2,1)S(1)}, u32[]{:S(2)}, u32[]{:S(2)}) %collective-permute-start.18) | collective-permute-done | bytes 208928 | tf_op jit(solution)/shard_map/ppermute | solution.py:35
  66.1 3.5 %collective-permute-start.19 = (bf16[128,384]{1,0:T(8,128)(2,1)S(1)}, bf16[128,384]{1,0:T(8,128)(2,1)S(1)}, u32[]{:S(2)}, u32[]{:S(2)}) collective-permute-start(bf16[128,384]{1,0:T(8,128)(2,1)S(1)} %slice.8), channel_id=1, source_target_pairs={{0,32},{32,64},{64,96},{96,128},{128,160},{160,192},{192,224},{224... | collective-permute-start | bytes 294920 | tf_op jit(solution)/shard_map/ppermute | solution.py:35
  69.6 2.1 %collective-permute-done.19.refs_7_ = bf16[128,384]{1,0:T(8,128)(2,1)S(1)} collective-permute-done((bf16[128,384]{1,0:T(8,128)(2,1)S(1)}, bf16[128,384]{1,0:T(8,128)(2,1)S(1)}, u32[]{:S(2)}, u32[]{:S(2)}) %collective-permute-start.19) | collective-permute-done | bytes 98336 | tf_op jit(solution)/shard_map/ppermute | solution.py:35
  72.3 1.8 %merge.1 = (bf16[128,2048]{1,0:T(8,128)(2,1)S(1)}, bf16[2048,256]{1,0:T(8,128)(2,1)S(1)}) custom-call(s32[2]{0:T(128)S(1)} %pad_add_fusion.place, bf16[272,384]{1,0:T(8,128)(2,1)S(1)} %finish_rows.1.refs_0_, bf16[272,384]{1,0:T(8,128)(2,1)S(1)} %collective-permute-done.13.refs_1_, bf16[272,384]{1,0:T(8,128)(2,1)S(1)} %collective-permute-done.14.refs_2_, ...), custom_call_target="tpu_custom_call" | custom-call | tf_op jit(solution)/shard_map/merge/pallas_call | solution.py:193
  74.1 4.8 %attend.7 = bf16[272,512]{1,0:T(8,128)(2,1)S(1)} custom-call(s32[2]{0:T(128)S(1)} %pad_add_fusion.place, bf16[128,2048]{1,0:T(8,128)(2,1)S(1)} %get-tuple-element.57.keys, bf16[2048,256]{1,0:T(8,128)(2,1)S(1)} %get-tuple-element.58.values, bf16[256,512]{1,0:T(8,128)(2,1)} %collective-permute-done.25.query_ref), custom_call_target="tpu_custom_call" | custom-call | flops 1073741824 | bytes 2097152 | tf_op jit(solution)/shard_map/attend/pallas_call | solution.py:279
  79.7 4.8 %attend.6 = bf16[272,512]{1,0:T(8,128)(2,1)S(1)} custom-call(s32[2]{0:T(128)S(1)} %pad_add_fusion.place, bf16[128,2048]{1,0:T(8,128)(2,1)S(1)} %get-tuple-element.57.keys, bf16[2048,256]{1,0:T(8,128)(2,1)S(1)} %get-tuple-element.58.values, bf16[256,512]{1,0:T(8,128)(2,1)} %collective-permute-done.23.query_ref), custom_call_target="tpu_custom_call" | custom-call | flops 1073741824 | bytes 2097152 | tf_op jit(solution)/shard_map/attend/pallas_call | solution.py:279
  86.2 4.8 %attend.5 = bf16[272,512]{1,0:T(8,128)(2,1)S(1)} custom-call(s32[2]{0:T(128)S(1)} %pad_add_fusion.place, bf16[128,2048]{1,0:T(8,128)(2,1)S(1)} %get-tuple-element.57.keys, bf16[2048,256]{1,0:T(8,128)(2,1)S(1)} %get-tuple-element.58.values, bf16[256,512]{1,0:T(8,128)(2,1)} %collective-permute-done.21.query_ref), custom_call_target="tpu_custom_call" | custom-call | flops 1073741824 | bytes 2097152 | tf_op jit(solution)/shard_map/attend/pallas_call | solution.py:279
  92.6 4.4 %attend.4.refs_0_ = bf16[272,512]{1,0:T(8,128)(2,1)S(1)} custom-call(s32[2]{0:T(128)S(1)} %pad_add_fusion.place, bf16[128,2048]{1,0:T(8,128)(2,1)S(1)} %get-tuple-element.57.keys, bf16[2048,256]{1,0:T(8,128)(2,1)S(1)} %get-tuple-element.58.values, bf16[256,512]{1,0:T(8,128)(2,1)S(1)} %copy-done.7), custom_call_target="tpu_custom_call" | custom-call | flops 1073741824 | bytes 2097152 | tf_op jit(solution)/shard_map/attend/pallas_call | solution.py:279
  97.1 2.1 %collective-permute-done.22.refs_1_ = bf16[272,512]{1,0:T(8,128)(2,1)S(1)} collective-permute-done((bf16[272,512]{1,0:T(8,128)(2,1)S(1)}, bf16[272,512]{1,0:T(8,128)(2,1)S(1)}, u32[]{:S(2)}, u32[]{:S(2)}) %collective-permute-start.22) | collective-permute-done | bytes 278560 | tf_op jit(solution)/shard_map/ppermute | solution.py:35
  (78 shorter events, 28.3 us)
Async XLA Ops:
  7.1 10.7 %collective-permute-start.1 = (bf16[64,1280]{1,0:T(8,128)(2,1)S(1)}, bf16[64,1280]{1,0:T(8,128)(2,1)}, u32[]{:S(2)}, u32[]{:S(2)}) collective-permute-start(bf16[64,1280]{1,0:T(8,128)(2,1)S(1)} %fusion.27), channel_id=1, source_target_pairs={{0,4},{2,6},{4,0},{6,2},{1,5},{3,7},{5,1},{7,3},{8,12},{10,14},{12... | collective-permute-start | bytes 491528 | tf_op jit(solution)/shard_map/ppermute | solution.py:35
  10.3 8.3 %collective-permute-start.2 = (bf16[64,1280]{1,0:T(8,128)(2,1)S(1)}, bf16[64,1280]{1,0:T(8,128)(2,1)}, u32[]{:S(2)}, u32[]{:S(2)}) collective-permute-start(bf16[64,1280]{1,0:T(8,128)(2,1)S(1)} %fusion.27), channel_id=1, source_target_pairs={{0,2},{2,4},{4,6},{6,0},{1,3},{3,5},{5,7},{7,1},{8,10},{10,12},{12... | collective-permute-start | bytes 491528 | tf_op jit(solution)/shard_map/ppermute | solution.py:35
  10.8 7.8 %collective-permute-start.3 = (bf16[64,1280]{1,0:T(8,128)(2,1)S(1)}, bf16[64,1280]{1,0:T(8,128)(2,1)}, u32[]{:S(2)}, u32[]{:S(2)}) collective-permute-start(bf16[64,1280]{1,0:T(8,128)(2,1)S(1)} %fusion.27), channel_id=1, source_target_pairs={{0,6},{2,0},{4,2},{6,4},{1,7},{3,1},{5,3},{7,5},{8,14},{10,8},{12,... | collective-permute-start | bytes 491528 | tf_op jit(solution)/shard_map/ppermute | solution.py:35
  20.1 5.5 %collective-permute-start.5 = (bf16[64,1280]{1,0:T(8,128)(2,1)S(1)}, bf16[64,1280]{1,0:T(8,128)(2,1)S(1)}, u32[]{:S(2)}, u32[]{:S(2)}) collective-permute-start(bf16[64,1280]{1,0:T(8,128)(2,1)S(1)} %fusion.11.half_ref), channel_id=1, source_target_pairs={{0,1},{1,0},{2,3},{3,2},{4,5},{5,4},{6,7},{7,6},{8,9},{9,8},{10,11... | collective-permute-start | bytes 491528 | tf_op jit(solution)/shard_map/ppermute | solution.py:35
  20.4 10.8 %collective-permute-start.6 = (bf16[272,256]{1,0:T(8,128)(2,1)S(1)}, bf16[272,256]{1,0:T(8,128)(2,1)S(1)}, u32[]{:S(2)}, u32[]{:S(2)}) collective-permute-start(bf16[272,256]{1,0:T(8,128)(2,1)S(1)} %get-tuple-element.44), channel_id=1, source_target_pairs={{0,4},{2,6},{4,0},{6,2},{1,5},{3,7},{5,1},{7,3},{8,12},{10,14},{12... | collective-permute-start | bytes 417800 | tf_op jit(solution)/shard_map/ppermute | solution.py:35
  22.4 8.8 %collective-permute-start.7 = (bf16[272,256]{1,0:T(8,128)(2,1)S(1)}, bf16[272,256]{1,0:T(8,128)(2,1)S(1)}, u32[]{:S(2)}, u32[]{:S(2)}) collective-permute-start(bf16[272,256]{1,0:T(8,128)(2,1)S(1)} %get-tuple-element.45), channel_id=1, source_target_pairs={{0,2},{2,4},{4,6},{6,0},{1,3},{3,5},{5,7},{7,1},{8,10},{10,12},{12... | collective-permute-start | bytes 417800 | tf_op jit(solution)/shard_map/ppermute | solution.py:35
  23.9 7.4 %collective-permute-start.8 = (bf16[272,256]{1,0:T(8,128)(2,1)S(1)}, bf16[272,256]{1,0:T(8,128)(2,1)S(1)}, u32[]{:S(2)}, u32[]{:S(2)}) collective-permute-start(bf16[272,256]{1,0:T(8,128)(2,1)S(1)} %get-tuple-element.46), channel_id=1, source_target_pairs={{0,6},{2,0},{4,2},{6,4},{1,7},{3,1},{5,3},{7,5},{8,14},{10,8},{12,... | collective-permute-start | bytes 417800 | tf_op jit(solution)/shard_map/ppermute | solution.py:35
  33.0 8.2 %collective-permute-start.10 = (bf16[272,128]{1,0:T(8,128)(2,1)S(1)}, bf16[272,128]{1,0:T(8,128)(2,1)S(1)}, u32[]{:S(2)}, u32[]{:S(2)}) collective-permute-start(bf16[272,128]{1,0:T(8,128)(2,1)S(1)} %get-tuple-element.54), channel_id=1, source_target_pairs={{0,4},{2,6},{4,0},{6,2},{1,5},{3,7},{5,1},{7,3},{8,12},{10,14},{12... | collective-permute-start | bytes 208904 | tf_op jit(solution)/shard_map/ppermute | solution.py:35
  34.7 8.5 %collective-permute-start.11 = (bf16[272,128]{1,0:T(8,128)(2,1)S(1)}, bf16[272,128]{1,0:T(8,128)(2,1)S(1)}, u32[]{:S(2)}, u32[]{:S(2)}) collective-permute-start(bf16[272,128]{1,0:T(8,128)(2,1)S(1)} %get-tuple-element.55), channel_id=1, source_target_pairs={{0,2},{2,4},{4,6},{6,0},{1,3},{3,5},{5,7},{7,1},{8,10},{10,12},{12... | collective-permute-start | bytes 208904 | tf_op jit(solution)/shard_map/ppermute | solution.py:35
  36.1 7.1 %collective-permute-start.12 = (bf16[272,128]{1,0:T(8,128)(2,1)S(1)}, bf16[272,128]{1,0:T(8,128)(2,1)S(1)}, u32[]{:S(2)}, u32[]{:S(2)}) collective-permute-start(bf16[272,128]{1,0:T(8,128)(2,1)S(1)} %get-tuple-element.56), channel_id=1, source_target_pairs={{0,6},{2,0},{4,2},{6,4},{1,7},{3,1},{5,3},{7,5},{8,14},{10,8},{12,... | collective-permute-start | bytes 208904 | tf_op jit(solution)/shard_map/ppermute | solution.py:35
  37.9 36.2 %collective-permute-start.25 = (bf16[256,512]{1,0:T(8,128)(2,1)S(1)}, bf16[256,512]{1,0:T(8,128)(2,1)}, u32[]{:S(2)}, u32[]{:S(2)}) collective-permute-start(bf16[256,512]{1,0:T(8,128)(2,1)S(1)} %copy-done.7), channel_id=1, source_target_pairs={{0,8},{8,16},{16,24},{24,0},{1,9},{9,17},{17,25},{25,1},{2,10},{10... | collective-permute-start | bytes 786440 | tf_op jit(solution)/shard_map/ppermute | solution.py:35
  39.5 40.2 %collective-permute-start.23 = (bf16[256,512]{1,0:T(8,128)(2,1)S(1)}, bf16[256,512]{1,0:T(8,128)(2,1)}, u32[]{:S(2)}, u32[]{:S(2)}) collective-permute-start(bf16[256,512]{1,0:T(8,128)(2,1)S(1)} %copy-done.7), channel_id=1, source_target_pairs={{0,24},{8,0},{16,8},{24,16},{1,25},{9,1},{17,9},{25,17},{2,26},{10... | collective-permute-start | bytes 786440 | tf_op jit(solution)/shard_map/ppermute | solution.py:35
  41.1 45.1 %collective-permute-start.21 = (bf16[256,512]{1,0:T(8,128)(2,1)S(1)}, bf16[256,512]{1,0:T(8,128)(2,1)}, u32[]{:S(2)}, u32[]{:S(2)}) collective-permute-start(bf16[256,512]{1,0:T(8,128)(2,1)S(1)} %copy-done.7), channel_id=1, source_target_pairs={{0,16},{8,24},{16,0},{24,8},{1,17},{9,25},{17,1},{25,9},{2,18},{10... | collective-permute-start | bytes 786440 | tf_op jit(solution)/shard_map/ppermute | solution.py:35
  43.8 7.1 %collective-permute-start.14 = (bf16[272,384]{1,0:T(8,128)(2,1)S(1)}, bf16[272,384]{1,0:T(8,128)(2,1)S(1)}, u32[]{:S(2)}, u32[]{:S(2)}) collective-permute-start(bf16[272,384]{1,0:T(8,128)(2,1)S(1)} %finish_rows.1.refs_0_), channel_id=1, source_target_pairs={{0,224},{32,0},{64,32},{96,64},{128,96},{160,128},{192,160},{224,1... | collective-permute-start | bytes 626696 | tf_op jit(solution)/shard_map/ppermute | solution.py:35
  44.9 6.0 %collective-permute-start.13 = (bf16[272,384]{1,0:T(8,128)(2,1)S(1)}, bf16[272,384]{1,0:T(8,128)(2,1)S(1)}, u32[]{:S(2)}, u32[]{:S(2)}) collective-permute-start(bf16[272,384]{1,0:T(8,128)(2,1)S(1)} %finish_rows.1.refs_0_), channel_id=1, source_target_pairs={{0,32},{32,64},{64,96},{96,128},{128,160},{160,192},{192,224},{224... | collective-permute-start | bytes 626696 | tf_op jit(solution)/shard_map/ppermute | solution.py:35
  50.9 7.0 %collective-permute-start.16 = (bf16[272,384]{1,0:T(8,128)(2,1)S(1)}, bf16[272,384]{1,0:T(8,128)(2,1)S(1)}, u32[]{:S(2)}, u32[]{:S(2)}) collective-permute-start(bf16[272,384]{1,0:T(8,128)(2,1)S(1)} %collective-permute-done.14.refs_2_), channel_id=1, source_target_pairs={{0,224},{32,0},{64,32},{96,64},{128,96},{160,128},{192,160},{224,1... | collective-permute-start | bytes 626696 | tf_op jit(solution)/shard_map/ppermute | solution.py:35
  50.9 7.0 %collective-permute-start.15 = (bf16[272,384]{1,0:T(8,128)(2,1)S(1)}, bf16[272,384]{1,0:T(8,128)(2,1)S(1)}, u32[]{:S(2)}, u32[]{:S(2)}) collective-permute-start(bf16[272,384]{1,0:T(8,128)(2,1)S(1)} %collective-permute-done.13.refs_1_), channel_id=1, source_target_pairs={{0,32},{32,64},{64,96},{96,128},{128,160},{160,192},{192,224},{224... | collective-permute-start | bytes 626696 | tf_op jit(solution)/shard_map/ppermute | solution.py:35
  57.9 8.0 %collective-permute-start.18 = (bf16[272,384]{1,0:T(8,128)(2,1)S(1)}, bf16[272,384]{1,0:T(8,128)(2,1)S(1)}, u32[]{:S(2)}, u32[]{:S(2)}) collective-permute-start(bf16[272,384]{1,0:T(8,128)(2,1)S(1)} %collective-permute-done.16.refs_4_), channel_id=1, source_target_pairs={{0,224},{32,0},{64,32},{96,64},{128,96},{160,128},{192,160},{224,1... | collective-permute-start | bytes 626696 | tf_op jit(solution)/shard_map/ppermute | solution.py:35
  57.9 8.1 %collective-permute-start.17 = (bf16[272,384]{1,0:T(8,128)(2,1)S(1)}, bf16[272,384]{1,0:T(8,128)(2,1)S(1)}, u32[]{:S(2)}, u32[]{:S(2)}) collective-permute-start(bf16[272,384]{1,0:T(8,128)(2,1)S(1)} %collective-permute-done.15.refs_3_), channel_id=1, source_target_pairs={{0,32},{32,64},{64,96},{96,128},{128,160},{160,192},{192,224},{224... | collective-permute-start | bytes 626696 | tf_op jit(solution)/shard_map/ppermute | solution.py:35
  66.0 6.0 %collective-permute-start.20 = (bf16[144,384]{1,0:T(8,128)(2,1)S(1)}, bf16[144,384]{1,0:T(8,128)(2,1)S(1)}, u32[]{:S(2)}, u32[]{:S(2)}) collective-permute-start(bf16[144,384]{1,0:T(8,128)(2,1)S(1)} %slice.9), channel_id=1, source_target_pairs={{0,224},{32,0},{64,32},{96,64},{128,96},{160,128},{192,160},{224,1... | collective-permute-start | bytes 331784 | tf_op jit(solution)/shard_map/ppermute | solution.py:35
  66.1 5.7 %collective-permute-start.19 = (bf16[128,384]{1,0:T(8,128)(2,1)S(1)}, bf16[128,384]{1,0:T(8,128)(2,1)S(1)}, u32[]{:S(2)}, u32[]{:S(2)}) collective-permute-start(bf16[128,384]{1,0:T(8,128)(2,1)S(1)} %slice.8), channel_id=1, source_target_pairs={{0,32},{32,64},{64,96},{96,128},{128,160},{160,192},{192,224},{224... | collective-permute-start | bytes 294920 | tf_op jit(solution)/shard_map/ppermute | solution.py:35
  79.0 18.1 %collective-permute-start.26 = (bf16[272,512]{1,0:T(8,128)(2,1)S(1)}, bf16[272,512]{1,0:T(8,128)(2,1)S(1)}, u32[]{:S(2)}, u32[]{:S(2)}) collective-permute-start(bf16[272,512]{1,0:T(8,128)(2,1)S(1)} %attend.7), channel_id=1, source_target_pairs={{0,24},{8,0},{16,8},{24,16},{1,25},{9,1},{17,9},{25,17},{2,26},{10... | collective-permute-start | bytes 835592 | tf_op jit(solution)/shard_map/ppermute | solution.py:35
  84.5 12.6 %collective-permute-start.24 = (bf16[272,512]{1,0:T(8,128)(2,1)S(1)}, bf16[272,512]{1,0:T(8,128)(2,1)S(1)}, u32[]{:S(2)}, u32[]{:S(2)}) collective-permute-start(bf16[272,512]{1,0:T(8,128)(2,1)S(1)} %attend.6), channel_id=1, source_target_pairs={{0,8},{8,16},{16,24},{24,0},{1,9},{9,17},{17,25},{25,1},{2,10},{10... | collective-permute-start | bytes 835592 | tf_op jit(solution)/shard_map/ppermute | solution.py:35
  91.1 8.1 %collective-permute-start.22 = (bf16[272,512]{1,0:T(8,128)(2,1)S(1)}, bf16[272,512]{1,0:T(8,128)(2,1)S(1)}, u32[]{:S(2)}, u32[]{:S(2)}) collective-permute-start(bf16[272,512]{1,0:T(8,128)(2,1)S(1)} %attend.5), channel_id=1, source_target_pairs={{0,16},{8,24},{16,0},{24,8},{1,17},{9,25},{17,1},{25,9},{2,18},{10... | collective-permute-start | bytes 835592 | tf_op jit(solution)/shard_map/ppermute | solution.py:35
  (13 other events, 78.2 us)

commit v2 on v1

--- a/solution.py
+++ b/solution.py
@@ -146,12 +146,13 @@
     )(slots, *text, *image)
 
 
-def ring_gather(block):
-    blocks, up, down = [block], block, block
-    for _ in range(3):
-        up, down = shift(up, Z, 1), shift(down, Z, 7)
-        blocks += [up, down]
-    return [*blocks, shift(up[:IMG], Z, 1), shift(down[IMG:], Z, 7)]
+def ring_gather(block, asked):
+    up1, down1 = shift(block, Z, 1), shift(block, Z, 7)
+    up2, down2 = shift(up1, Z, 1), shift(down1, Z, 7)
+    up2, down2, asked = lax.optimization_barrier((up2, down2, asked))
+    up3, down3 = shift(up2, Z, 1), shift(down2, Z, 7)
+    far = [shift(up2[:IMG], Z, 2), shift(down2[IMG:], Z, 6)]
+    return [block, up1, down1, up2, down2, up3, down3, *far], asked
 
 
 def exchange(pieces):
@@ -384,8 +385,8 @@
     )
     give, keep, text_got = lax.optimization_barrier((give, keep, text_got))
     image_got = exchange(add_pair(keep, shift(give, "core", 1), x_at))
-    blocks = ring_gather(finish_rows(slot_source, text_got, image_got))
     asked = {step: shift(queries, "y", 4 - step) for step in (2, 1, 3)}
+    blocks, asked = ring_gather(finish_rows(slot_source, text_got, image_got), asked)
 
     frequencies = jnp.exp(
         jnp.arange(HALF, dtype=F32) * (-2.0 * math.log(500000.0) / (2 * HALF))

time: 101 us -> 103 us (1.020); the launches traced: 101 us -> 101 us
  starting transfers between devices: 39.8 us -> 36.8 us
  waiting for transfers between devices: 19.9 us -> 22.5 us
    ppermute x27, starting transfers between devices: 39.8 us -> 36.8 us  [shift(): lax.ppermute(values, axis, [(i, (i + step) % count) for i in range(count)])]
    ppermute x27, waiting for transfers between devices: 19.9 us -> 22.5 us  [shift(): lax.ppermute(values, axis, [(i, (i + step) % count) for i in range(count)])]
    unnamed x20 -> x24, local copies, waits for them, and re-layouts: 6.15 us -> 6.85 us
  transfers between devices with their start and end apart: 27 -> 27, of which waited for: 10 -> 10; matrix products, arithmetic and copies ran while one was open for 2% -> 2% of each run, Pallas kernels for 25% -> 9%
where the time goes in v2:
time: 103 us; the launch traced here: 101 us
  starting transfers between devices  36.8 us (36%)
  Pallas kernels  26.7 us (26%)
  waiting for transfers between devices  22.5 us (22%)
  local copies, waits for them, and re-layouts  7.15 us (7%)
  other arithmetic  4.29 us (4%)
  matrix products  3.08 us (3%)
    ppermute x27, starting transfers between devices, shift(): lax.ppermute(values, axis, [(i, (i + step) % count) for i in range(count)])  36.8 us
    ppermute x27, waiting for transfers between devices, shift(): lax.ppermute(values, axis, [(i, (i + step) % count) for i in range(count)])  22.5 us
    pallas_call x4, Pallas kernels, attend(): pl.pallas_call(functools.partial(attend_kernel, step), out_shape=jax.Shap...  18.8 us
    unnamed x24, local copies, waits for them, and re-layouts  6.85 us
    pallas_call x2, Pallas kernels, project(): pl.pallas_call(kernel, out_shape=(shape, shape), in_specs=[pl.BlockSpec(m...  3.75 us
    dot_general x1, matrix products, body(): jnp.dot(enc_hidden, encoder_down, preferred_element_type=F32).astype(BF16)  3.08 us
  transfers between devices with their start and end apart: 27, of which 10 were waited for; matrix products, arithmetic and copies ran while one was open for 2% of the time, Pallas kernels for 9%

profile of v2, /device:TPU:224, one launch (start us, length us, event | category | flops | bytes accessed | tf_op | source)
XLA Modules:
  0.0 100.8 jit_solution(2242165711266283531)
XLA Ops:
  2.5 3.1 %convolution_convert_fusion = bf16[128,1280]{1,0:T(8,128)(2,1)S(1)} fusion(bf16[640,1280]{1,0:T(8,128)(2,1)S(1)} %copy-done, bf16[1280,640]{1,0:T(8,128)(2,1)} %param.14, bf16[128,1280]{1,0:T(8,128)(2,1)} %param.11, f32[1280]{0:T(1024)} %param.13, f32[1280]{0:T(1024)} %param.12, f32[128]{0:T(128)S(1)} %add_rsqrt_fusion, f32[128]{0:T(128)S(1)} %broadcast_multiply_fusion), kind=kOutput, calls=%fused_computation | convolution fusion | flops 425902080 | bytes 3943424 | tf_op jit(solution)/shard_map/dot_general | solution.py:362
  7.1 2.8 %collective-permute-start.3 = (bf16[64,1280]{1,0:T(8,128)(2,1)S(1)}, bf16[64,1280]{1,0:T(8,128)(2,1)}, u32[]{:S(2)}, u32[]{:S(2)}) collective-permute-start(bf16[64,1280]{1,0:T(8,128)(2,1)S(1)} %fusion.27), channel_id=1, source_target_pairs={{0,6},{2,0},{4,2},{6,4},{1,7},{3,1},{5,3},{7,5},{8,14},{10,8},{12,... | collective-permute-start | bytes 491528 | tf_op jit(solution)/shard_map/ppermute | solution.py:35
  10.0 2.3 %collective-permute-start.1 = (bf16[64,1280]{1,0:T(8,128)(2,1)S(1)}, bf16[64,1280]{1,0:T(8,128)(2,1)}, u32[]{:S(2)}, u32[]{:S(2)}) collective-permute-start(bf16[64,1280]{1,0:T(8,128)(2,1)S(1)} %fusion.27), channel_id=1, source_target_pairs={{0,4},{2,6},{4,0},{6,2},{1,5},{3,7},{5,1},{7,3},{8,12},{10,14},{12... | collective-permute-start | bytes 491528 | tf_op jit(solution)/shard_map/ppermute | solution.py:35
  12.3 2.2 %copy-done.1 = bf16[2048,1024]{1,0:T(8,128)(2,1)S(1)} copy-done((bf16[2048,1024]{1,0:T(8,128)(2,1)S(1)}, bf16[2048,1024]{1,0:T(8,128)(2,1)}, u32[]{:S(2)}) %copy-start.1) | copy-done | bytes 4194328
  14.5 2.1 %project.2 = (bf16[4,272,256]{2,1,0:T(8,128)(2,1)}, bf16[4,272,256]{2,1,0:T(8,128)(2,1)S(1)}) custom-call(s32[1]{0:T(128)} %bitcast.2.core, bf16[256,1024]{1,0:T(8,128)(2,1)S(1)} %copy-done.4, f32[1,1024]{1,0:T(1,128)S(1)} %bitcast.18, bf16[2048,1024]{1,0:T(8,128)(2,1)S(1)} %copy-done.1), custom_call_target="tpu_custom_call" | custom-call | tf_op jit(solution)/shard_map/project/pallas_call | solution.py:90
  17.3 3.5 %collective-permute-done.2 = bf16[64,1280]{1,0:T(8,128)(2,1)} collective-permute-done((bf16[64,1280]{1,0:T(8,128)(2,1)S(1)}, bf16[64,1280]{1,0:T(8,128)(2,1)}, u32[]{:S(2)}, u32[]{:S(2)}) %collective-permute-start.2) | collective-permute-done | bytes 163872 | tf_op jit(solution)/shard_map/ppermute | solution.py:35
  23.6 2.7 %collective-permute-start.8 = (bf16[272,256]{1,0:T(8,128)(2,1)S(1)}, bf16[272,256]{1,0:T(8,128)(2,1)S(1)}, u32[]{:S(2)}, u32[]{:S(2)}) collective-permute-start(bf16[272,256]{1,0:T(8,128)(2,1)S(1)} %get-tuple-element.51), channel_id=1, source_target_pairs={{0,6},{2,0},{4,2},{6,4},{1,7},{3,1},{5,3},{7,5},{8,14},{10,8},{12,... | collective-permute-start | bytes 417800 | tf_op jit(solution)/shard_map/ppermute | solution.py:35
  26.2 2.2 %copy-done.2 = bf16[2048,1024]{1,0:T(8,128)(2,1)S(1)} copy-done((bf16[2048,1024]{1,0:T(8,128)(2,1)S(1)}, bf16[2048,1024]{1,0:T(8,128)(2,1)}, u32[]{:S(2)}) %copy-start.2) | copy-done | bytes 4194328
  36.1 2.5 %collective-permute-start.12 = (bf16[272,128]{1,0:T(8,128)(2,1)S(1)}, bf16[272,128]{1,0:T(8,128)(2,1)S(1)}, u32[]{:S(2)}, u32[]{:S(2)}) collective-permute-start(bf16[272,128]{1,0:T(8,128)(2,1)S(1)} %get-tuple-element.61), channel_id=1, source_target_pairs={{0,6},{2,0},{4,2},{6,4},{1,7},{3,1},{5,3},{7,5},{8,14},{10,8},{12,... | collective-permute-start | bytes 208904 | tf_op jit(solution)/shard_map/ppermute | solution.py:35
  38.6 3.2 %collective-permute-start.18 = (bf16[256,512]{1,0:T(8,128)(2,1)S(1)}, bf16[256,512]{1,0:T(8,128)(2,1)}, u32[]{:S(2)}, u32[]{:S(2)}) collective-permute-start(bf16[256,512]{1,0:T(8,128)(2,1)S(1)} %copy-done.7), channel_id=1, source_target_pairs={{0,16},{8,24},{16,0},{24,8},{1,17},{9,25},{17,1},{25,9},{2,18},{10... | collective-permute-start | bytes 786440 | tf_op jit(solution)/shard_map/ppermute | solution.py:35
  45.6 2.2 %collective-permute-start.13 = (bf16[272,384]{1,0:T(8,128)(2,1)S(1)}, bf16[272,384]{1,0:T(8,128)(2,1)S(1)}, u32[]{:S(2)}, u32[]{:S(2)}) collective-permute-start(bf16[272,384]{1,0:T(8,128)(2,1)S(1)} %finish_rows.1.refs_0_), channel_id=1, source_target_pairs={{0,32},{32,64},{64,96},{96,128},{128,160},{160,192},{192,224},{224... | collective-permute-start | bytes 626696 | tf_op jit(solution)/shard_map/ppermute | solution.py:35
  47.8 3.8 %collective-permute-done.14.refs_2_ = bf16[272,384]{1,0:T(8,128)(2,1)S(1)} collective-permute-done((bf16[272,384]{1,0:T(8,128)(2,1)S(1)}, bf16[272,384]{1,0:T(8,128)(2,1)S(1)}, u32[]{:S(2)}, u32[]{:S(2)}) %collective-permute-start.14) | collective-permute-done | bytes 208928 | tf_op jit(solution)/shard_map/ppermute | solution.py:35
  51.6 3.2 %collective-permute-start.15 = (bf16[272,384]{1,0:T(8,128)(2,1)S(1)}, bf16[272,384]{1,0:T(8,128)(2,1)S(1)}, u32[]{:S(2)}, u32[]{:S(2)}) collective-permute-start(bf16[272,384]{1,0:T(8,128)(2,1)S(1)} %collective-permute-done.13.refs_1_), channel_id=1, source_target_pairs={{0,32},{32,64},{64,96},{96,128},{128,160},{160,192},{192,224},{224... | collective-permute-start | bytes 626696 | tf_op jit(solution)/shard_map/ppermute | solution.py:35
  55.9 2.7 %collective-permute-done.16.refs_4_ = bf16[272,384]{1,0:T(8,128)(2,1)S(1)} collective-permute-done((bf16[272,384]{1,0:T(8,128)(2,1)S(1)}, bf16[272,384]{1,0:T(8,128)(2,1)S(1)}, u32[]{:S(2)}, u32[]{:S(2)}) %collective-permute-start.16) | collective-permute-done | bytes 208928 | tf_op jit(solution)/shard_map/ppermute | solution.py:35
  58.6 3.2 %collective-permute-start.20 = (bf16[272,384]{1,0:T(8,128)(2,1)S(1)}, bf16[272,384]{1,0:T(8,128)(2,1)S(1)}, u32[]{:S(2)}, u32[]{:S(2)}) collective-permute-start(bf16[272,384]{1,0:T(8,128)(2,1)S(1)} %collective-permute-done.15.refs_3_), channel_id=1, source_target_pairs={{0,32},{32,64},{64,96},{96,128},{128,160},{160,192},{192,224},{224... | collective-permute-start | bytes 626696 | tf_op jit(solution)/shard_map/ppermute | solution.py:35
  65.1 2.7 %collective-permute-done.22.refs_7_ = bf16[128,384]{1,0:T(8,128)(2,1)S(1)} collective-permute-done((bf16[128,384]{1,0:T(8,128)(2,1)S(1)}, bf16[128,384]{1,0:T(8,128)(2,1)S(1)}, u32[]{:S(2)}, u32[]{:S(2)}) %collective-permute-start.22) | collective-permute-done | bytes 98336 | tf_op jit(solution)/shard_map/ppermute | solution.py:35
  67.8 3.9 %collective-permute-done.23.refs_8_ = bf16[144,384]{1,0:T(8,128)(2,1)S(1)} collective-permute-done((bf16[144,384]{1,0:T(8,128)(2,1)S(1)}, bf16[144,384]{1,0:T(8,128)(2,1)S(1)}, u32[]{:S(2)}, u32[]{:S(2)}) %collective-permute-start.23) | collective-permute-done | bytes 110624 | tf_op jit(solution)/shard_map/ppermute | solution.py:35
  71.9 1.8 %merge.1 = (bf16[128,2048]{1,0:T(8,128)(2,1)S(1)}, bf16[2048,256]{1,0:T(8,128)(2,1)S(1)}) custom-call(s32[2]{0:T(128)S(1)} %pad_add_fusion.place, bf16[272,384]{1,0:T(8,128)(2,1)S(1)} %finish_rows.1.refs_0_, bf16[272,384]{1,0:T(8,128)(2,1)S(1)} %collective-permute-done.13.refs_1_, bf16[272,384]{1,0:T(8,128)(2,1)S(1)} %collective-permute-done.14.refs_2_, ...), custom_call_target="tpu_custom_call" | custom-call | tf_op jit(solution)/shard_map/merge/pallas_call | solution.py:194
  73.8 4.4 %attend.7 = bf16[272,512]{1,0:T(8,128)(2,1)S(1)} custom-call(s32[2]{0:T(128)S(1)} %pad_add_fusion.place, bf16[128,2048]{1,0:T(8,128)(2,1)S(1)} %get-tuple-element.64.keys, bf16[2048,256]{1,0:T(8,128)(2,1)S(1)} %get-tuple-element.65.values, bf16[256,512]{1,0:T(8,128)(2,1)S(1)} %copy-done.9), custom_call_target="tpu_custom_call" | custom-call | flops 1073741824 | bytes 2097152 | tf_op jit(solution)/shard_map/attend/pallas_call | solution.py:280
  78.2 5.1 %attend.6 = bf16[272,512]{1,0:T(8,128)(2,1)S(1)} custom-call(s32[2]{0:T(128)S(1)} %pad_add_fusion.place, bf16[128,2048]{1,0:T(8,128)(2,1)S(1)} %get-tuple-element.64.keys, bf16[2048,256]{1,0:T(8,128)(2,1)S(1)} %get-tuple-element.65.values, bf16[256,512]{1,0:T(8,128)(2,1)} %collective-permute-done.17.query_ref), custom_call_target="tpu_custom_call" | custom-call | flops 1073741824 | bytes 2097152 | tf_op jit(solution)/shard_map/attend/pallas_call | solution.py:280
  83.3 4.8 %attend.5 = bf16[272,512]{1,0:T(8,128)(2,1)S(1)} custom-call(s32[2]{0:T(128)S(1)} %pad_add_fusion.place, bf16[128,2048]{1,0:T(8,128)(2,1)S(1)} %get-tuple-element.64.keys, bf16[2048,256]{1,0:T(8,128)(2,1)S(1)} %get-tuple-element.65.values, bf16[256,512]{1,0:T(8,128)(2,1)} %collective-permute-done.18.query_ref), custom_call_target="tpu_custom_call" | custom-call | flops 1073741824 | bytes 2097152 | tf_op jit(solution)/shard_map/attend/pallas_call | solution.py:280
  88.1 2.3 %collective-permute-start.24 = (bf16[272,512]{1,0:T(8,128)(2,1)S(1)}, bf16[272,512]{1,0:T(8,128)(2,1)S(1)}, u32[]{:S(2)}, u32[]{:S(2)}) collective-permute-start(bf16[272,512]{1,0:T(8,128)(2,1)S(1)} %attend.5), channel_id=1, source_target_pairs={{0,16},{8,24},{16,0},{24,8},{1,17},{9,25},{17,1},{25,9},{2,18},{10... | collective-permute-start | bytes 835592 | tf_op jit(solution)/shard_map/ppermute | solution.py:35
  91.4 2.3 %collective-permute-start.26 = (bf16[272,512]{1,0:T(8,128)(2,1)S(1)}, bf16[272,512]{1,0:T(8,128)(2,1)S(1)}, u32[]{:S(2)}, u32[]{:S(2)}) collective-permute-start(bf16[272,512]{1,0:T(8,128)(2,1)S(1)} %attend.7), channel_id=1, source_target_pairs={{0,24},{8,0},{16,8},{24,16},{1,25},{9,1},{17,9},{25,17},{2,26},{10... | collective-permute-start | bytes 835592 | tf_op jit(solution)/shard_map/ppermute | solution.py:35
  93.7 4.4 %attend.4.refs_0_ = bf16[272,512]{1,0:T(8,128)(2,1)S(1)} custom-call(s32[2]{0:T(128)S(1)} %pad_add_fusion.place, bf16[128,2048]{1,0:T(8,128)(2,1)S(1)} %get-tuple-element.64.keys, bf16[2048,256]{1,0:T(8,128)(2,1)S(1)} %get-tuple-element.65.values, bf16[256,512]{1,0:T(8,128)(2,1)S(1)} %copy-done.7), custom_call_target="tpu_custom_call" | custom-call | flops 1073741824 | bytes 2097152 | tf_op jit(solution)/shard_map/attend/pallas_call | solution.py:280
  (82 shorter events, 27.1 us)
Async XLA Ops:
  7.1 10.1 %collective-permute-start.3 = (bf16[64,1280]{1,0:T(8,128)(2,1)S(1)}, bf16[64,1280]{1,0:T(8,128)(2,1)}, u32[]{:S(2)}, u32[]{:S(2)}) collective-permute-start(bf16[64,1280]{1,0:T(8,128)(2,1)S(1)} %fusion.27), channel_id=1, source_target_pairs={{0,6},{2,0},{4,2},{6,4},{1,7},{3,1},{5,3},{7,5},{8,14},{10,8},{12,... | collective-permute-start | bytes 491528 | tf_op jit(solution)/shard_map/ppermute | solution.py:35
  10.0 10.8 %collective-permute-start.2 = (bf16[64,1280]{1,0:T(8,128)(2,1)S(1)}, bf16[64,1280]{1,0:T(8,128)(2,1)}, u32[]{:S(2)}, u32[]{:S(2)}) collective-permute-start(bf16[64,1280]{1,0:T(8,128)(2,1)S(1)} %fusion.27), channel_id=1, source_target_pairs={{0,2},{2,4},{4,6},{6,0},{1,3},{3,5},{5,7},{7,1},{8,10},{10,12},{12... | collective-permute-start | bytes 491528 | tf_op jit(solution)/shard_map/ppermute | solution.py:35
  10.0 10.8 %collective-permute-start.1 = (bf16[64,1280]{1,0:T(8,128)(2,1)S(1)}, bf16[64,1280]{1,0:T(8,128)(2,1)}, u32[]{:S(2)}, u32[]{:S(2)}) collective-permute-start(bf16[64,1280]{1,0:T(8,128)(2,1)S(1)} %fusion.27), channel_id=1, source_target_pairs={{0,4},{2,6},{4,0},{6,2},{1,5},{3,7},{5,1},{7,3},{8,12},{10,14},{12... | collective-permute-start | bytes 491528 | tf_op jit(solution)/shard_map/ppermute | solution.py:35
  16.6 5.5 %collective-permute-start.4 = (bf16[4,272,256]{2,1,0:T(8,128)(2,1)}, bf16[4,272,256]{2,1,0:T(8,128)(2,1)S(1)}, u32[]{:S(2)}, u32[]{:S(2)}) collective-permute-start(bf16[4,272,256]{2,1,0:T(8,128)(2,1)} %get-tuple-element.40), channel_id=1, source_target_pairs={{0,1},{1,0},{2,3},{3,2},{4,5},{5,4},{6,7},{7,6},{8,9},{9,8},{10,11... | collective-permute-start | bytes 1671176 | tf_op jit(solution)/shard_map/ppermute | solution.py:35
  22.3 9.5 %collective-permute-start.6 = (bf16[272,256]{1,0:T(8,128)(2,1)S(1)}, bf16[272,256]{1,0:T(8,128)(2,1)S(1)}, u32[]{:S(2)}, u32[]{:S(2)}) collective-permute-start(bf16[272,256]{1,0:T(8,128)(2,1)S(1)} %get-tuple-element.49), channel_id=1, source_target_pairs={{0,4},{2,6},{4,0},{6,2},{1,5},{3,7},{5,1},{7,3},{8,12},{10,14},{12... | collective-permute-start | bytes 417800 | tf_op jit(solution)/shard_map/ppermute | solution.py:35
  23.0 9.9 %collective-permute-start.7 = (bf16[272,256]{1,0:T(8,128)(2,1)S(1)}, bf16[272,256]{1,0:T(8,128)(2,1)S(1)}, u32[]{:S(2)}, u32[]{:S(2)}) collective-permute-start(bf16[272,256]{1,0:T(8,128)(2,1)S(1)} %get-tuple-element.50), channel_id=1, source_target_pairs={{0,2},{2,4},{4,6},{6,0},{1,3},{3,5},{5,7},{7,1},{8,10},{10,12},{12... | collective-permute-start | bytes 417800 | tf_op jit(solution)/shard_map/ppermute | solution.py:35
  23.6 9.3 %collective-permute-start.8 = (bf16[272,256]{1,0:T(8,128)(2,1)S(1)}, bf16[272,256]{1,0:T(8,128)(2,1)S(1)}, u32[]{:S(2)}, u32[]{:S(2)}) collective-permute-start(bf16[272,256]{1,0:T(8,128)(2,1)S(1)} %get-tuple-element.51), channel_id=1, source_target_pairs={{0,6},{2,0},{4,2},{6,4},{1,7},{3,1},{5,3},{7,5},{8,14},{10,8},{12,... | collective-permute-start | bytes 417800 | tf_op jit(solution)/shard_map/ppermute | solution.py:35
  34.5 8.3 %collective-permute-start.10 = (bf16[272,128]{1,0:T(8,128)(2,1)S(1)}, bf16[272,128]{1,0:T(8,128)(2,1)S(1)}, u32[]{:S(2)}, u32[]{:S(2)}) collective-permute-start(bf16[272,128]{1,0:T(8,128)(2,1)S(1)} %get-tuple-element.59), channel_id=1, source_target_pairs={{0,4},{2,6},{4,0},{6,2},{1,5},{3,7},{5,1},{7,3},{8,12},{10,14},{12... | collective-permute-start | bytes 208904 | tf_op jit(solution)/shard_map/ppermute | solution.py:35
  35.4 8.5 %collective-permute-start.11 = (bf16[272,128]{1,0:T(8,128)(2,1)S(1)}, bf16[272,128]{1,0:T(8,128)(2,1)S(1)}, u32[]{:S(2)}, u32[]{:S(2)}) collective-permute-start(bf16[272,128]{1,0:T(8,128)(2,1)S(1)} %get-tuple-element.60), channel_id=1, source_target_pairs={{0,2},{2,4},{4,6},{6,0},{1,3},{3,5},{5,7},{7,1},{8,10},{10,12},{12... | collective-permute-start | bytes 208904 | tf_op jit(solution)/shard_map/ppermute | solution.py:35
  36.1 7.7 %collective-permute-start.12 = (bf16[272,128]{1,0:T(8,128)(2,1)S(1)}, bf16[272,128]{1,0:T(8,128)(2,1)S(1)}, u32[]{:S(2)}, u32[]{:S(2)}) collective-permute-start(bf16[272,128]{1,0:T(8,128)(2,1)S(1)} %get-tuple-element.61), channel_id=1, source_target_pairs={{0,6},{2,0},{4,2},{6,4},{1,7},{3,1},{5,3},{7,5},{8,14},{10,8},{12,... | collective-permute-start | bytes 208904 | tf_op jit(solution)/shard_map/ppermute | solution.py:35
  38.6 16.6 %collective-permute-start.18 = (bf16[256,512]{1,0:T(8,128)(2,1)S(1)}, bf16[256,512]{1,0:T(8,128)(2,1)}, u32[]{:S(2)}, u32[]{:S(2)}) collective-permute-start(bf16[256,512]{1,0:T(8,128)(2,1)S(1)} %copy-done.7), channel_id=1, source_target_pairs={{0,16},{8,24},{16,0},{24,8},{1,17},{9,25},{17,1},{25,9},{2,18},{10... | collective-permute-start | bytes 786440 | tf_op jit(solution)/shard_map/ppermute | solution.py:35
  41.8 13.4 %collective-permute-start.17 = (bf16[256,512]{1,0:T(8,128)(2,1)S(1)}, bf16[256,512]{1,0:T(8,128)(2,1)}, u32[]{:S(2)}, u32[]{:S(2)}) collective-permute-start(bf16[256,512]{1,0:T(8,128)(2,1)S(1)} %copy-done.7), channel_id=1, source_target_pairs={{0,24},{8,0},{16,8},{24,16},{1,25},{9,1},{17,9},{25,17},{2,26},{10... | collective-permute-start | bytes 786440 | tf_op jit(solution)/shard_map/ppermute | solution.py:35
  42.9 12.3 %collective-permute-start.19 = (bf16[256,512]{1,0:T(8,128)(2,1)S(1)}, bf16[256,512]{1,0:T(8,128)(2,1)S(1)}, u32[]{:S(2)}, u32[]{:S(2)}) collective-permute-start(bf16[256,512]{1,0:T(8,128)(2,1)S(1)} %copy-done.7), channel_id=1, source_target_pairs={{0,8},{8,16},{16,24},{24,0},{1,9},{9,17},{17,25},{25,1},{2,10},{10... | collective-permute-start | bytes 786440 | tf_op jit(solution)/shard_map/ppermute | solution.py:35
  44.5 7.1 %collective-permute-start.14 = (bf16[272,384]{1,0:T(8,128)(2,1)S(1)}, bf16[272,384]{1,0:T(8,128)(2,1)S(1)}, u32[]{:S(2)}, u32[]{:S(2)}) collective-permute-start(bf16[272,384]{1,0:T(8,128)(2,1)S(1)} %finish_rows.1.refs_0_), channel_id=1, source_target_pairs={{0,224},{32,0},{64,32},{96,64},{128,96},{160,128},{192,160},{224,1... | collective-permute-start | bytes 626696 | tf_op jit(solution)/shard_map/ppermute | solution.py:35
  45.6 6.0 %collective-permute-start.13 = (bf16[272,384]{1,0:T(8,128)(2,1)S(1)}, bf16[272,384]{1,0:T(8,128)(2,1)S(1)}, u32[]{:S(2)}, u32[]{:S(2)}) collective-permute-start(bf16[272,384]{1,0:T(8,128)(2,1)S(1)} %finish_rows.1.refs_0_), channel_id=1, source_target_pairs={{0,32},{32,64},{64,96},{96,128},{128,160},{160,192},{192,224},{224... | collective-permute-start | bytes 626696 | tf_op jit(solution)/shard_map/ppermute | solution.py:35
  51.6 7.0 %collective-permute-start.16 = (bf16[272,384]{1,0:T(8,128)(2,1)S(1)}, bf16[272,384]{1,0:T(8,128)(2,1)S(1)}, u32[]{:S(2)}, u32[]{:S(2)}) collective-permute-start(bf16[272,384]{1,0:T(8,128)(2,1)S(1)} %collective-permute-done.14.refs_2_), channel_id=1, source_target_pairs={{0,224},{32,0},{64,32},{96,64},{128,96},{160,128},{192,160},{224,1... | collective-permute-start | bytes 626696 | tf_op jit(solution)/shard_map/ppermute | solution.py:35
  51.6 7.0 %collective-permute-start.15 = (bf16[272,384]{1,0:T(8,128)(2,1)S(1)}, bf16[272,384]{1,0:T(8,128)(2,1)S(1)}, u32[]{:S(2)}, u32[]{:S(2)}) collective-permute-start(bf16[272,384]{1,0:T(8,128)(2,1)S(1)} %collective-permute-done.13.refs_1_), channel_id=1, source_target_pairs={{0,32},{32,64},{64,96},{96,128},{128,160},{160,192},{192,224},{224... | collective-permute-start | bytes 626696 | tf_op jit(solution)/shard_map/ppermute | solution.py:35
  58.6 13.1 %collective-permute-start.20 = (bf16[272,384]{1,0:T(8,128)(2,1)S(1)}, bf16[272,384]{1,0:T(8,128)(2,1)S(1)}, u32[]{:S(2)}, u32[]{:S(2)}) collective-permute-start(bf16[272,384]{1,0:T(8,128)(2,1)S(1)} %collective-permute-done.15.refs_3_), channel_id=1, source_target_pairs={{0,32},{32,64},{64,96},{96,128},{128,160},{160,192},{192,224},{224... | collective-permute-start | bytes 626696 | tf_op jit(solution)/shard_map/ppermute | solution.py:35
  61.9 9.8 %collective-permute-start.21 = (bf16[272,384]{1,0:T(8,128)(2,1)S(1)}, bf16[272,384]{1,0:T(8,128)(2,1)S(1)}, u32[]{:S(2)}, u32[]{:S(2)}) collective-permute-start(bf16[272,384]{1,0:T(8,128)(2,1)S(1)} %collective-permute-done.16.refs_4_), channel_id=1, source_target_pairs={{0,224},{32,0},{64,32},{96,64},{128,96},{160,128},{192,160},{224,1... | collective-permute-start | bytes 626696 | tf_op jit(solution)/shard_map/ppermute | solution.py:35
  62.0 5.7 %collective-permute-start.22 = (bf16[128,384]{1,0:T(8,128)(2,1)S(1)}, bf16[128,384]{1,0:T(8,128)(2,1)S(1)}, u32[]{:S(2)}, u32[]{:S(2)}) collective-permute-start(bf16[128,384]{1,0:T(8,128)(2,1)S(1)} %slice.6), channel_id=1, source_target_pairs={{0,64},{32,96},{64,128},{96,160},{128,192},{160,224},{192,0},{224,... | collective-permute-start | bytes 294920 | tf_op jit(solution)/shard_map/ppermute | solution.py:35
  63.6 8.1 %collective-permute-start.23 = (bf16[144,384]{1,0:T(8,128)(2,1)S(1)}, bf16[144,384]{1,0:T(8,128)(2,1)S(1)}, u32[]{:S(2)}, u32[]{:S(2)}) collective-permute-start(bf16[144,384]{1,0:T(8,128)(2,1)S(1)} %slice.7), channel_id=1, source_target_pairs={{0,192},{32,224},{64,0},{96,32},{128,64},{160,96},{192,128},{224,1... | collective-permute-start | bytes 331784 | tf_op jit(solution)/shard_map/ppermute | solution.py:35
  88.1 10.0 %collective-permute-start.24 = (bf16[272,512]{1,0:T(8,128)(2,1)S(1)}, bf16[272,512]{1,0:T(8,128)(2,1)S(1)}, u32[]{:S(2)}, u32[]{:S(2)}) collective-permute-start(bf16[272,512]{1,0:T(8,128)(2,1)S(1)} %attend.5), channel_id=1, source_target_pairs={{0,16},{8,24},{16,0},{24,8},{1,17},{9,25},{17,1},{25,9},{2,18},{10... | collective-permute-start | bytes 835592 | tf_op jit(solution)/shard_map/ppermute | solution.py:35
  90.4 8.9 %collective-permute-start.25 = (bf16[272,512]{1,0:T(8,128)(2,1)S(1)}, bf16[272,512]{1,0:T(8,128)(2,1)S(1)}, u32[]{:S(2)}, u32[]{:S(2)}) collective-permute-start(bf16[272,512]{1,0:T(8,128)(2,1)S(1)} %attend.6), channel_id=1, source_target_pairs={{0,8},{8,16},{16,24},{24,0},{1,9},{9,17},{17,25},{25,1},{2,10},{10... | collective-permute-start | bytes 835592 | tf_op jit(solution)/shard_map/ppermute | solution.py:35
  91.4 8.0 %collective-permute-start.26 = (bf16[272,512]{1,0:T(8,128)(2,1)S(1)}, bf16[272,512]{1,0:T(8,128)(2,1)S(1)}, u32[]{:S(2)}, u32[]{:S(2)}) collective-permute-start(bf16[272,512]{1,0:T(8,128)(2,1)S(1)} %attend.7), channel_id=1, source_target_pairs={{0,24},{8,0},{16,8},{24,16},{1,25},{9,1},{17,9},{25,17},{2,26},{10... | collective-permute-start | bytes 835592 | tf_op jit(solution)/shard_map/ppermute | solution.py:35
  (15 other events, 90.8 us)

commit v3 on v1

--- a/solution.py
+++ b/solution.py
@@ -209,31 +209,41 @@
 def attend_kernel(step, place, keys, values, query_ref, out_ref, scores, top, mixed):
     z_at, y_at = place[0], place[1]
     block_at = lax.rem(y_at + step, 4)
+    full = z_at + jnp.where(y_at < block_at, 1, 0)
     count = z_at + jnp.where(y_at <= block_at, 1, 0)
+    plain = full // PER
     chunks = (count + PER - 1) // PER
     top[...] = jnp.full(top.shape, NEG, F32)
 
     def chunk_at(chunk, offset=0, size=CHUNK):
         return pl.ds(pl.multiple_of(chunk * CHUNK + offset, HEAD), size)
 
-    key_at = lax.broadcasted_iota(jnp.int32, (TOK, CHUNK), 1)
-    reach = lax.broadcasted_iota(jnp.int32, (TOK, CHUNK), 0) - key_at - (key_at // TOK) * (3 * TOK)
-
-    @pl.loop(0, chunks)
-    def score(chunk):
+    def score(chunk, masked):
         keys_now = keys[:, chunk_at(chunk)]
-        allowed = reach >= ((PER * chunk - z_at) * 4 + y_at - block_at) * TOK
+        if masked:
+            key_at = lax.broadcasted_iota(jnp.int32, (TOK, CHUNK), 1)
+            key_at = key_at + (key_at // TOK) * (3 * TOK)
+            query_at = lax.broadcasted_iota(jnp.int32, (TOK, CHUNK), 0)
+            offset = ((PER * chunk - z_at) * 4 + y_at - block_at) * TOK
+            allowed = key_at + offset <= query_at
         for h in range(GROUP):
             here = slice(h * TOK, (h + 1) * TOK)
             s = jnp.dot(
                 query_ref[:, h * HEAD : (h + 1) * HEAD], keys_now, preferred_element_type=F32
             )
-            s = jnp.where(allowed, s, -jnp.inf)
+            if masked:
+                s = jnp.where(allowed, s, -jnp.inf)
             scores[here, chunk_at(chunk)] = s
             most = top[here, :]
             for lane in range(0, CHUNK, HEAD):
                 most = jnp.maximum(most, s[:, lane : lane + HEAD])
             top[here, :] = most
+
+    pl.loop(0, plain)(lambda chunk: score(chunk, False))
+
+    @pl.when(chunks > plain)
+    def last():
+        score(plain, True)
 
     top[...] = jnp.broadcast_to(jnp.max(top[...], axis=1, keepdims=True), top.shape)
 

time: 101 us -> 101 us (level)
  transfers between devices with their start and end apart: 27 -> 27, of which waited for: 10 -> 10; matrix products, arithmetic and copies ran while one was open for 2% -> 2% of each run, Pallas kernels for 25% -> 24%
where the time goes in v3:
time: 101 us; the launch traced here: 100 us
  starting transfers between devices  40.1 us (40%)
  Pallas kernels  26.2 us (26%)
  waiting for transfers between devices  19.8 us (20%)
  local copies, waits for them, and re-layouts  6.44 us (6%)
  other arithmetic  4.29 us (4%)
  matrix products  3.08 us (3%)
    ppermute x27, starting transfers between devices, shift(): lax.ppermute(values, axis, [(i, (i + step) % count) for i in range(count)])  40.1 us
    ppermute x27, waiting for transfers between devices, shift(): lax.ppermute(values, axis, [(i, (i + step) % count) for i in range(count)])  19.8 us
    pallas_call x4, Pallas kernels, attend(): pl.pallas_call(functools.partial(attend_kernel, step), out_shape=jax.Shap...  18.2 us
    unnamed x20, local copies, waits for them, and re-layouts  6.15 us
    pallas_call x2, Pallas kernels, project(): pl.pallas_call(kernel, out_shape=(shape, shape), in_specs=[pl.BlockSpec(m...  3.77 us
    dot_general x1, matrix products, body(): jnp.dot(enc_hidden, encoder_down, preferred_element_type=F32).astype(BF16)  3.08 us
  transfers between devices with their start and end apart: 27, of which 10 were waited for; matrix products, arithmetic and copies ran while one was open for 2% of the time, Pallas kernels for 24%

profile of v3, /device:TPU:224, one launch (start us, length us, event | category | flops | bytes accessed | tf_op | source)
XLA Modules:
  0.0 100.1 jit_solution(5109153362980697194)
XLA Ops:
  2.5 3.1 %convolution_convert_fusion = bf16[128,1280]{1,0:T(8,128)(2,1)S(1)} fusion(bf16[640,1280]{1,0:T(8,128)(2,1)S(1)} %copy-done, bf16[1280,640]{1,0:T(8,128)(2,1)} %param.14, bf16[128,1280]{1,0:T(8,128)(2,1)} %param.11, f32[1280]{0:T(1024)} %param.13, f32[1280]{0:T(1024)} %param.12, f32[128]{0:T(128)S(1)} %add_rsqrt_fusion, f32[128]{0:T(128)S(1)} %broadcast_multiply_fusion), kind=kOutput, calls=%fused_computation | convolution fusion | flops 425902080 | bytes 3943424 | tf_op jit(solution)/shard_map/dot_general | solution.py:371
  7.1 3.1 %collective-permute-start.1 = (bf16[64,1280]{1,0:T(8,128)(2,1)S(1)}, bf16[64,1280]{1,0:T(8,128)(2,1)}, u32[]{:S(2)}, u32[]{:S(2)}) collective-permute-start(bf16[64,1280]{1,0:T(8,128)(2,1)S(1)} %fusion.27), channel_id=1, source_target_pairs={{0,4},{2,6},{4,0},{6,2},{1,5},{3,7},{5,1},{7,3},{8,12},{10,14},{12... | collective-permute-start | bytes 491528 | tf_op jit(solution)/shard_map/ppermute | solution.py:35
  10.8 2.6 %collective-permute-start.3 = (bf16[64,1280]{1,0:T(8,128)(2,1)S(1)}, bf16[64,1280]{1,0:T(8,128)(2,1)}, u32[]{:S(2)}, u32[]{:S(2)}) collective-permute-start(bf16[64,1280]{1,0:T(8,128)(2,1)S(1)} %fusion.27), channel_id=1, source_target_pairs={{0,6},{2,0},{4,2},{6,4},{1,7},{3,1},{5,3},{7,5},{8,14},{10,8},{12,... | collective-permute-start | bytes 491528 | tf_op jit(solution)/shard_map/ppermute | solution.py:35
  13.5 2.2 %copy-done.1 = bf16[2048,1024]{1,0:T(8,128)(2,1)S(1)} copy-done((bf16[2048,1024]{1,0:T(8,128)(2,1)S(1)}, bf16[2048,1024]{1,0:T(8,128)(2,1)}, u32[]{:S(2)}) %copy-start.1) | copy-done | bytes 4194328
  15.7 2.1 %project.2 = (bf16[4,272,256]{2,1,0:T(8,128)(2,1)}, bf16[4,272,256]{2,1,0:T(8,128)(2,1)S(1)}) custom-call(s32[1]{0:T(128)} %bitcast.2.core, bf16[256,1024]{1,0:T(8,128)(2,1)S(1)} %copy-done.4, f32[1,1024]{1,0:T(1,128)S(1)} %bitcast.18, bf16[2048,1024]{1,0:T(8,128)(2,1)S(1)} %copy-done.1), custom_call_target="tpu_custom_call" | custom-call | tf_op jit(solution)/shard_map/project/pallas_call | solution.py:90
  20.4 2.0 %collective-permute-start.6 = (bf16[272,256]{1,0:T(8,128)(2,1)S(1)}, bf16[272,256]{1,0:T(8,128)(2,1)S(1)}, u32[]{:S(2)}, u32[]{:S(2)}) collective-permute-start(bf16[272,256]{1,0:T(8,128)(2,1)S(1)} %get-tuple-element.44), channel_id=1, source_target_pairs={{0,4},{2,6},{4,0},{6,2},{1,5},{3,7},{5,1},{7,3},{8,12},{10,14},{12... | collective-permute-start | bytes 417800 | tf_op jit(solution)/shard_map/ppermute | solution.py:35
  25.6 2.2 %copy-done.2 = bf16[2048,1024]{1,0:T(8,128)(2,1)S(1)} copy-done((bf16[2048,1024]{1,0:T(8,128)(2,1)S(1)}, bf16[2048,1024]{1,0:T(8,128)(2,1)}, u32[]{:S(2)}) %copy-start.2) | copy-done | bytes 4194328
  36.1 1.8 %collective-permute-start.12 = (bf16[272,128]{1,0:T(8,128)(2,1)S(1)}, bf16[272,128]{1,0:T(8,128)(2,1)S(1)}, u32[]{:S(2)}, u32[]{:S(2)}) collective-permute-start(bf16[272,128]{1,0:T(8,128)(2,1)S(1)} %get-tuple-element.56), channel_id=1, source_target_pairs={{0,6},{2,0},{4,2},{6,4},{1,7},{3,1},{5,3},{7,5},{8,14},{10,8},{12,... | collective-permute-start | bytes 208904 | tf_op jit(solution)/shard_map/ppermute | solution.py:35
  41.1 2.0 %collective-permute-start.21 = (bf16[256,512]{1,0:T(8,128)(2,1)S(1)}, bf16[256,512]{1,0:T(8,128)(2,1)}, u32[]{:S(2)}, u32[]{:S(2)}) collective-permute-start(bf16[256,512]{1,0:T(8,128)(2,1)S(1)} %copy-done.7), channel_id=1, source_target_pairs={{0,16},{8,24},{16,0},{24,8},{1,17},{9,25},{17,1},{25,9},{2,18},{10... | collective-permute-start | bytes 786440 | tf_op jit(solution)/shard_map/ppermute | solution.py:35
  44.9 2.2 %collective-permute-start.13 = (bf16[272,384]{1,0:T(8,128)(2,1)S(1)}, bf16[272,384]{1,0:T(8,128)(2,1)S(1)}, u32[]{:S(2)}, u32[]{:S(2)}) collective-permute-start(bf16[272,384]{1,0:T(8,128)(2,1)S(1)} %finish_rows.1.refs_0_), channel_id=1, source_target_pairs={{0,32},{32,64},{64,96},{96,128},{128,160},{160,192},{192,224},{224... | collective-permute-start | bytes 626696 | tf_op jit(solution)/shard_map/ppermute | solution.py:35
  47.1 3.8 %collective-permute-done.14.refs_2_ = bf16[272,384]{1,0:T(8,128)(2,1)S(1)} collective-permute-done((bf16[272,384]{1,0:T(8,128)(2,1)S(1)}, bf16[272,384]{1,0:T(8,128)(2,1)S(1)}, u32[]{:S(2)}, u32[]{:S(2)}) %collective-permute-start.14) | collective-permute-done | bytes 208928 | tf_op jit(solution)/shard_map/ppermute | solution.py:35
  50.9 3.2 %collective-permute-start.15 = (bf16[272,384]{1,0:T(8,128)(2,1)S(1)}, bf16[272,384]{1,0:T(8,128)(2,1)S(1)}, u32[]{:S(2)}, u32[]{:S(2)}) collective-permute-start(bf16[272,384]{1,0:T(8,128)(2,1)S(1)} %collective-permute-done.13.refs_1_), channel_id=1, source_target_pairs={{0,32},{32,64},{64,96},{96,128},{128,160},{160,192},{192,224},{224... | collective-permute-start | bytes 626696 | tf_op jit(solution)/shard_map/ppermute | solution.py:35
  54.5 3.5 %collective-permute-done.16.refs_4_ = bf16[272,384]{1,0:T(8,128)(2,1)S(1)} collective-permute-done((bf16[272,384]{1,0:T(8,128)(2,1)S(1)}, bf16[272,384]{1,0:T(8,128)(2,1)S(1)}, u32[]{:S(2)}, u32[]{:S(2)}) %collective-permute-start.16) | collective-permute-done | bytes 208928 | tf_op jit(solution)/shard_map/ppermute | solution.py:35
  57.9 3.5 %collective-permute-start.17 = (bf16[272,384]{1,0:T(8,128)(2,1)S(1)}, bf16[272,384]{1,0:T(8,128)(2,1)S(1)}, u32[]{:S(2)}, u32[]{:S(2)}) collective-permute-start(bf16[272,384]{1,0:T(8,128)(2,1)S(1)} %collective-permute-done.15.refs_3_), channel_id=1, source_target_pairs={{0,32},{32,64},{64,96},{96,128},{128,160},{160,192},{192,224},{224... | collective-permute-start | bytes 626696 | tf_op jit(solution)/shard_map/ppermute | solution.py:35
  61.5 4.4 %collective-permute-done.18.refs_6_ = bf16[272,384]{1,0:T(8,128)(2,1)S(1)} collective-permute-done((bf16[272,384]{1,0:T(8,128)(2,1)S(1)}, bf16[272,384]{1,0:T(8,128)(2,1)S(1)}, u32[]{:S(2)}, u32[]{:S(2)}) %collective-permute-start.18) | collective-permute-done | bytes 208928 | tf_op jit(solution)/shard_map/ppermute | solution.py:35
  66.1 3.5 %collective-permute-start.19 = (bf16[128,384]{1,0:T(8,128)(2,1)S(1)}, bf16[128,384]{1,0:T(8,128)(2,1)S(1)}, u32[]{:S(2)}, u32[]{:S(2)}) collective-permute-start(bf16[128,384]{1,0:T(8,128)(2,1)S(1)} %slice.8), channel_id=1, source_target_pairs={{0,32},{32,64},{64,96},{96,128},{128,160},{160,192},{192,224},{224... | collective-permute-start | bytes 294920 | tf_op jit(solution)/shard_map/ppermute | solution.py:35
  69.6 2.1 %collective-permute-done.19.refs_7_ = bf16[128,384]{1,0:T(8,128)(2,1)S(1)} collective-permute-done((bf16[128,384]{1,0:T(8,128)(2,1)S(1)}, bf16[128,384]{1,0:T(8,128)(2,1)S(1)}, u32[]{:S(2)}, u32[]{:S(2)}) %collective-permute-start.19) | collective-permute-done | bytes 98336 | tf_op jit(solution)/shard_map/ppermute | solution.py:35
  72.3 1.8 %merge.1 = (bf16[128,2048]{1,0:T(8,128)(2,1)S(1)}, bf16[2048,256]{1,0:T(8,128)(2,1)S(1)}) custom-call(s32[2]{0:T(128)S(1)} %pad_add_fusion.place, bf16[272,384]{1,0:T(8,128)(2,1)S(1)} %finish_rows.1.refs_0_, bf16[272,384]{1,0:T(8,128)(2,1)S(1)} %collective-permute-done.13.refs_1_, bf16[272,384]{1,0:T(8,128)(2,1)S(1)} %collective-permute-done.14.refs_2_, ...), custom_call_target="tpu_custom_call" | custom-call | tf_op jit(solution)/shard_map/merge/pallas_call | solution.py:193
  74.1 4.6 %attend.7 = bf16[272,512]{1,0:T(8,128)(2,1)S(1)} custom-call(s32[2]{0:T(128)S(1)} %pad_add_fusion.place, bf16[128,2048]{1,0:T(8,128)(2,1)S(1)} %get-tuple-element.57.keys, bf16[2048,256]{1,0:T(8,128)(2,1)S(1)} %get-tuple-element.58.values, bf16[256,512]{1,0:T(8,128)(2,1)} %collective-permute-done.25.query_ref), custom_call_target="tpu_custom_call" | custom-call | flops 1073741824 | bytes 2097152 | tf_op jit(solution)/shard_map/attend/pallas_call | solution.py:289
  79.6 4.6 %attend.6 = bf16[272,512]{1,0:T(8,128)(2,1)S(1)} custom-call(s32[2]{0:T(128)S(1)} %pad_add_fusion.place, bf16[128,2048]{1,0:T(8,128)(2,1)S(1)} %get-tuple-element.57.keys, bf16[2048,256]{1,0:T(8,128)(2,1)S(1)} %get-tuple-element.58.values, bf16[256,512]{1,0:T(8,128)(2,1)} %collective-permute-done.23.query_ref), custom_call_target="tpu_custom_call" | custom-call | flops 1073741824 | bytes 2097152 | tf_op jit(solution)/shard_map/attend/pallas_call | solution.py:289
  85.8 4.6 %attend.5 = bf16[272,512]{1,0:T(8,128)(2,1)S(1)} custom-call(s32[2]{0:T(128)S(1)} %pad_add_fusion.place, bf16[128,2048]{1,0:T(8,128)(2,1)S(1)} %get-tuple-element.57.keys, bf16[2048,256]{1,0:T(8,128)(2,1)S(1)} %get-tuple-element.58.values, bf16[256,512]{1,0:T(8,128)(2,1)} %collective-permute-done.21.query_ref), custom_call_target="tpu_custom_call" | custom-call | flops 1073741824 | bytes 2097152 | tf_op jit(solution)/shard_map/attend/pallas_call | solution.py:289
  90.5 1.9 %collective-permute-start.22 = (bf16[272,512]{1,0:T(8,128)(2,1)S(1)}, bf16[272,512]{1,0:T(8,128)(2,1)S(1)}, u32[]{:S(2)}, u32[]{:S(2)}) collective-permute-start(bf16[272,512]{1,0:T(8,128)(2,1)S(1)} %attend.5), channel_id=1, source_target_pairs={{0,16},{8,24},{16,0},{24,8},{1,17},{9,25},{17,1},{25,9},{2,18},{10... | collective-permute-start | bytes 835592 | tf_op jit(solution)/shard_map/ppermute | solution.py:35
  92.3 4.3 %attend.4.refs_0_ = bf16[272,512]{1,0:T(8,128)(2,1)S(1)} custom-call(s32[2]{0:T(128)S(1)} %pad_add_fusion.place, bf16[128,2048]{1,0:T(8,128)(2,1)S(1)} %get-tuple-element.57.keys, bf16[2048,256]{1,0:T(8,128)(2,1)S(1)} %get-tuple-element.58.values, bf16[256,512]{1,0:T(8,128)(2,1)S(1)} %copy-done.7), custom_call_target="tpu_custom_call" | custom-call | flops 1073741824 | bytes 2097152 | tf_op jit(solution)/shard_map/attend/pallas_call | solution.py:289
  96.7 1.9 %collective-permute-done.22.refs_1_ = bf16[272,512]{1,0:T(8,128)(2,1)S(1)} collective-permute-done((bf16[272,512]{1,0:T(8,128)(2,1)S(1)}, bf16[272,512]{1,0:T(8,128)(2,1)S(1)}, u32[]{:S(2)}, u32[]{:S(2)}) %collective-permute-start.22) | collective-permute-done | bytes 278560 | tf_op jit(solution)/shard_map/ppermute | solution.py:35
  (78 shorter events, 28.5 us)
Async XLA Ops:
  7.1 10.7 %collective-permute-start.1 = (bf16[64,1280]{1,0:T(8,128)(2,1)S(1)}, bf16[64,1280]{1,0:T(8,128)(2,1)}, u32[]{:S(2)}, u32[]{:S(2)}) collective-permute-start(bf16[64,1280]{1,0:T(8,128)(2,1)S(1)} %fusion.27), channel_id=1, source_target_pairs={{0,4},{2,6},{4,0},{6,2},{1,5},{3,7},{5,1},{7,3},{8,12},{10,14},{12... | collective-permute-start | bytes 491528 | tf_op jit(solution)/shard_map/ppermute | solution.py:35
  10.3 8.3 %collective-permute-start.2 = (bf16[64,1280]{1,0:T(8,128)(2,1)S(1)}, bf16[64,1280]{1,0:T(8,128)(2,1)}, u32[]{:S(2)}, u32[]{:S(2)}) collective-permute-start(bf16[64,1280]{1,0:T(8,128)(2,1)S(1)} %fusion.27), channel_id=1, source_target_pairs={{0,2},{2,4},{4,6},{6,0},{1,3},{3,5},{5,7},{7,1},{8,10},{10,12},{12... | collective-permute-start | bytes 491528 | tf_op jit(solution)/shard_map/ppermute | solution.py:35
  10.8 7.8 %collective-permute-start.3 = (bf16[64,1280]{1,0:T(8,128)(2,1)S(1)}, bf16[64,1280]{1,0:T(8,128)(2,1)}, u32[]{:S(2)}, u32[]{:S(2)}) collective-permute-start(bf16[64,1280]{1,0:T(8,128)(2,1)S(1)} %fusion.27), channel_id=1, source_target_pairs={{0,6},{2,0},{4,2},{6,4},{1,7},{3,1},{5,3},{7,5},{8,14},{10,8},{12,... | collective-permute-start | bytes 491528 | tf_op jit(solution)/shard_map/ppermute | solution.py:35
  20.1 5.5 %collective-permute-start.5 = (bf16[64,1280]{1,0:T(8,128)(2,1)S(1)}, bf16[64,1280]{1,0:T(8,128)(2,1)S(1)}, u32[]{:S(2)}, u32[]{:S(2)}) collective-permute-start(bf16[64,1280]{1,0:T(8,128)(2,1)S(1)} %fusion.11.half_ref), channel_id=1, source_target_pairs={{0,1},{1,0},{2,3},{3,2},{4,5},{5,4},{6,7},{7,6},{8,9},{9,8},{10,11... | collective-permute-start | bytes 491528 | tf_op jit(solution)/shard_map/ppermute | solution.py:35
  20.4 10.8 %collective-permute-start.6 = (bf16[272,256]{1,0:T(8,128)(2,1)S(1)}, bf16[272,256]{1,0:T(8,128)(2,1)S(1)}, u32[]{:S(2)}, u32[]{:S(2)}) collective-permute-start(bf16[272,256]{1,0:T(8,128)(2,1)S(1)} %get-tuple-element.44), channel_id=1, source_target_pairs={{0,4},{2,6},{4,0},{6,2},{1,5},{3,7},{5,1},{7,3},{8,12},{10,14},{12... | collective-permute-start | bytes 417800 | tf_op jit(solution)/shard_map/ppermute | solution.py:35
  22.4 8.8 %collective-permute-start.7 = (bf16[272,256]{1,0:T(8,128)(2,1)S(1)}, bf16[272,256]{1,0:T(8,128)(2,1)S(1)}, u32[]{:S(2)}, u32[]{:S(2)}) collective-permute-start(bf16[272,256]{1,0:T(8,128)(2,1)S(1)} %get-tuple-element.45), channel_id=1, source_target_pairs={{0,2},{2,4},{4,6},{6,0},{1,3},{3,5},{5,7},{7,1},{8,10},{10,12},{12... | collective-permute-start | bytes 417800 | tf_op jit(solution)/shard_map/ppermute | solution.py:35
  23.9 7.4 %collective-permute-start.8 = (bf16[272,256]{1,0:T(8,128)(2,1)S(1)}, bf16[272,256]{1,0:T(8,128)(2,1)S(1)}, u32[]{:S(2)}, u32[]{:S(2)}) collective-permute-start(bf16[272,256]{1,0:T(8,128)(2,1)S(1)} %get-tuple-element.46), channel_id=1, source_target_pairs={{0,6},{2,0},{4,2},{6,4},{1,7},{3,1},{5,3},{7,5},{8,14},{10,8},{12,... | collective-permute-start | bytes 417800 | tf_op jit(solution)/shard_map/ppermute | solution.py:35
  33.0 8.2 %collective-permute-start.10 = (bf16[272,128]{1,0:T(8,128)(2,1)S(1)}, bf16[272,128]{1,0:T(8,128)(2,1)S(1)}, u32[]{:S(2)}, u32[]{:S(2)}) collective-permute-start(bf16[272,128]{1,0:T(8,128)(2,1)S(1)} %get-tuple-element.54), channel_id=1, source_target_pairs={{0,4},{2,6},{4,0},{6,2},{1,5},{3,7},{5,1},{7,3},{8,12},{10,14},{12... | collective-permute-start | bytes 208904 | tf_op jit(solution)/shard_map/ppermute | solution.py:35
  34.7 8.5 %collective-permute-start.11 = (bf16[272,128]{1,0:T(8,128)(2,1)S(1)}, bf16[272,128]{1,0:T(8,128)(2,1)S(1)}, u32[]{:S(2)}, u32[]{:S(2)}) collective-permute-start(bf16[272,128]{1,0:T(8,128)(2,1)S(1)} %get-tuple-element.55), channel_id=1, source_target_pairs={{0,2},{2,4},{4,6},{6,0},{1,3},{3,5},{5,7},{7,1},{8,10},{10,12},{12... | collective-permute-start | bytes 208904 | tf_op jit(solution)/shard_map/ppermute | solution.py:35
  36.1 7.1 %collective-permute-start.12 = (bf16[272,128]{1,0:T(8,128)(2,1)S(1)}, bf16[272,128]{1,0:T(8,128)(2,1)S(1)}, u32[]{:S(2)}, u32[]{:S(2)}) collective-permute-start(bf16[272,128]{1,0:T(8,128)(2,1)S(1)} %get-tuple-element.56), channel_id=1, source_target_pairs={{0,6},{2,0},{4,2},{6,4},{1,7},{3,1},{5,3},{7,5},{8,14},{10,8},{12,... | collective-permute-start | bytes 208904 | tf_op jit(solution)/shard_map/ppermute | solution.py:35
  37.9 36.2 %collective-permute-start.25 = (bf16[256,512]{1,0:T(8,128)(2,1)S(1)}, bf16[256,512]{1,0:T(8,128)(2,1)}, u32[]{:S(2)}, u32[]{:S(2)}) collective-permute-start(bf16[256,512]{1,0:T(8,128)(2,1)S(1)} %copy-done.7), channel_id=1, source_target_pairs={{0,8},{8,16},{16,24},{24,0},{1,9},{9,17},{17,25},{25,1},{2,10},{10... | collective-permute-start | bytes 786440 | tf_op jit(solution)/shard_map/ppermute | solution.py:35
  39.5 40.1 %collective-permute-start.23 = (bf16[256,512]{1,0:T(8,128)(2,1)S(1)}, bf16[256,512]{1,0:T(8,128)(2,1)}, u32[]{:S(2)}, u32[]{:S(2)}) collective-permute-start(bf16[256,512]{1,0:T(8,128)(2,1)S(1)} %copy-done.7), channel_id=1, source_target_pairs={{0,24},{8,0},{16,8},{24,16},{1,25},{9,1},{17,9},{25,17},{2,26},{10... | collective-permute-start | bytes 786440 | tf_op jit(solution)/shard_map/ppermute | solution.py:35
  41.1 44.7 %collective-permute-start.21 = (bf16[256,512]{1,0:T(8,128)(2,1)S(1)}, bf16[256,512]{1,0:T(8,128)(2,1)}, u32[]{:S(2)}, u32[]{:S(2)}) collective-permute-start(bf16[256,512]{1,0:T(8,128)(2,1)S(1)} %copy-done.7), channel_id=1, source_target_pairs={{0,16},{8,24},{16,0},{24,8},{1,17},{9,25},{17,1},{25,9},{2,18},{10... | collective-permute-start | bytes 786440 | tf_op jit(solution)/shard_map/ppermute | solution.py:35
  43.8 7.1 %collective-permute-start.14 = (bf16[272,384]{1,0:T(8,128)(2,1)S(1)}, bf16[272,384]{1,0:T(8,128)(2,1)S(1)}, u32[]{:S(2)}, u32[]{:S(2)}) collective-permute-start(bf16[272,384]{1,0:T(8,128)(2,1)S(1)} %finish_rows.1.refs_0_), channel_id=1, source_target_pairs={{0,224},{32,0},{64,32},{96,64},{128,96},{160,128},{192,160},{224,1... | collective-permute-start | bytes 626696 | tf_op jit(solution)/shard_map/ppermute | solution.py:35
  44.9 6.0 %collective-permute-start.13 = (bf16[272,384]{1,0:T(8,128)(2,1)S(1)}, bf16[272,384]{1,0:T(8,128)(2,1)S(1)}, u32[]{:S(2)}, u32[]{:S(2)}) collective-permute-start(bf16[272,384]{1,0:T(8,128)(2,1)S(1)} %finish_rows.1.refs_0_), channel_id=1, source_target_pairs={{0,32},{32,64},{64,96},{96,128},{128,160},{160,192},{192,224},{224... | collective-permute-start | bytes 626696 | tf_op jit(solution)/shard_map/ppermute | solution.py:35
  50.9 7.0 %collective-permute-start.16 = (bf16[272,384]{1,0:T(8,128)(2,1)S(1)}, bf16[272,384]{1,0:T(8,128)(2,1)S(1)}, u32[]{:S(2)}, u32[]{:S(2)}) collective-permute-start(bf16[272,384]{1,0:T(8,128)(2,1)S(1)} %collective-permute-done.14.refs_2_), channel_id=1, source_target_pairs={{0,224},{32,0},{64,32},{96,64},{128,96},{160,128},{192,160},{224,1... | collective-permute-start | bytes 626696 | tf_op jit(solution)/shard_map/ppermute | solution.py:35
  50.9 7.0 %collective-permute-start.15 = (bf16[272,384]{1,0:T(8,128)(2,1)S(1)}, bf16[272,384]{1,0:T(8,128)(2,1)S(1)}, u32[]{:S(2)}, u32[]{:S(2)}) collective-permute-start(bf16[272,384]{1,0:T(8,128)(2,1)S(1)} %collective-permute-done.13.refs_1_), channel_id=1, source_target_pairs={{0,32},{32,64},{64,96},{96,128},{128,160},{160,192},{192,224},{224... | collective-permute-start | bytes 626696 | tf_op jit(solution)/shard_map/ppermute | solution.py:35
  57.9 8.0 %collective-permute-start.18 = (bf16[272,384]{1,0:T(8,128)(2,1)S(1)}, bf16[272,384]{1,0:T(8,128)(2,1)S(1)}, u32[]{:S(2)}, u32[]{:S(2)}) collective-permute-start(bf16[272,384]{1,0:T(8,128)(2,1)S(1)} %collective-permute-done.16.refs_4_), channel_id=1, source_target_pairs={{0,224},{32,0},{64,32},{96,64},{128,96},{160,128},{192,160},{224,1... | collective-permute-start | bytes 626696 | tf_op jit(solution)/shard_map/ppermute | solution.py:35
  57.9 8.1 %collective-permute-start.17 = (bf16[272,384]{1,0:T(8,128)(2,1)S(1)}, bf16[272,384]{1,0:T(8,128)(2,1)S(1)}, u32[]{:S(2)}, u32[]{:S(2)}) collective-permute-start(bf16[272,384]{1,0:T(8,128)(2,1)S(1)} %collective-permute-done.15.refs_3_), channel_id=1, source_target_pairs={{0,32},{32,64},{64,96},{96,128},{128,160},{160,192},{192,224},{224... | collective-permute-start | bytes 626696 | tf_op jit(solution)/shard_map/ppermute | solution.py:35
  66.0 6.0 %collective-permute-start.20 = (bf16[144,384]{1,0:T(8,128)(2,1)S(1)}, bf16[144,384]{1,0:T(8,128)(2,1)S(1)}, u32[]{:S(2)}, u32[]{:S(2)}) collective-permute-start(bf16[144,384]{1,0:T(8,128)(2,1)S(1)} %slice.9), channel_id=1, source_target_pairs={{0,224},{32,0},{64,32},{96,64},{128,96},{160,128},{192,160},{224,1... | collective-permute-start | bytes 331784 | tf_op jit(solution)/shard_map/ppermute | solution.py:35
  66.1 5.7 %collective-permute-start.19 = (bf16[128,384]{1,0:T(8,128)(2,1)S(1)}, bf16[128,384]{1,0:T(8,128)(2,1)S(1)}, u32[]{:S(2)}, u32[]{:S(2)}) collective-permute-start(bf16[128,384]{1,0:T(8,128)(2,1)S(1)} %slice.8), channel_id=1, source_target_pairs={{0,32},{32,64},{64,96},{96,128},{128,160},{160,192},{192,224},{224... | collective-permute-start | bytes 294920 | tf_op jit(solution)/shard_map/ppermute | solution.py:35
  78.8 17.9 %collective-permute-start.26 = (bf16[272,512]{1,0:T(8,128)(2,1)S(1)}, bf16[272,512]{1,0:T(8,128)(2,1)S(1)}, u32[]{:S(2)}, u32[]{:S(2)}) collective-permute-start(bf16[272,512]{1,0:T(8,128)(2,1)S(1)} %attend.7), channel_id=1, source_target_pairs={{0,24},{8,0},{16,8},{24,16},{1,25},{9,1},{17,9},{25,17},{2,26},{10... | collective-permute-start | bytes 835592 | tf_op jit(solution)/shard_map/ppermute | solution.py:35
  84.3 12.4 %collective-permute-start.24 = (bf16[272,512]{1,0:T(8,128)(2,1)S(1)}, bf16[272,512]{1,0:T(8,128)(2,1)S(1)}, u32[]{:S(2)}, u32[]{:S(2)}) collective-permute-start(bf16[272,512]{1,0:T(8,128)(2,1)S(1)} %attend.6), channel_id=1, source_target_pairs={{0,8},{8,16},{16,24},{24,0},{1,9},{9,17},{17,25},{25,1},{2,10},{10... | collective-permute-start | bytes 835592 | tf_op jit(solution)/shard_map/ppermute | solution.py:35
  90.5 8.1 %collective-permute-start.22 = (bf16[272,512]{1,0:T(8,128)(2,1)S(1)}, bf16[272,512]{1,0:T(8,128)(2,1)S(1)}, u32[]{:S(2)}, u32[]{:S(2)}) collective-permute-start(bf16[272,512]{1,0:T(8,128)(2,1)S(1)} %attend.5), channel_id=1, source_target_pairs={{0,16},{8,24},{16,0},{24,8},{1,17},{9,25},{17,1},{25,9},{2,18},{10... | collective-permute-start | bytes 835592 | tf_op jit(solution)/shard_map/ppermute | solution.py:35
  (13 other events, 78.2 us)

commit v4 on v3

--- a/solution.py
+++ b/solution.py
@@ -394,8 +394,10 @@
     )
     give, keep, text_got = lax.optimization_barrier((give, keep, text_got))
     image_got = exchange(add_pair(keep, shift(give, "core", 1), x_at))
-    blocks = ring_gather(finish_rows(slot_source, text_got, image_got))
-    asked = {step: shift(queries, "y", 4 - step) for step in (2, 1, 3)}
+    block = finish_rows(slot_source, text_got, image_got)
+    block, queries_later = lax.optimization_barrier((block, queries))
+    blocks = ring_gather(block)
+    asked = {step: shift(queries_later, "y", 4 - step) for step in (2, 1, 3)}
 
     frequencies = jnp.exp(
         jnp.arange(HALF, dtype=F32) * (-2.0 * math.log(500000.0) / (2 * HALF))

time: 101 us -> 101 us (level)
  starting transfers between devices: 40.1 us -> 38.5 us
  waiting for transfers between devices: 19.8 us -> 21.1 us
    ppermute x27, starting transfers between devices: 40.1 us -> 38.5 us  [shift(): lax.ppermute(values, axis, [(i, (i + step) % count) for i in range(count)])]
    ppermute x27, waiting for transfers between devices: 19.8 us -> 21.1 us  [shift(): lax.ppermute(values, axis, [(i, (i + step) % count) for i in range(count)])]
    unnamed x20 -> x22, local copies, waits for them, and re-layouts: 6.15 us -> 6.15 us
  transfers between devices with their start and end apart: 27 -> 27, of which waited for: 10 -> 11; matrix products, arithmetic and copies ran while one was open for 2% -> 2% of each run, Pallas kernels for 24% -> 23%
where the time goes in v4:
time: 101 us; the launch traced here: 100 us
  starting transfers between devices  38.5 us (38%)
  Pallas kernels  25.8 us (26%)
  waiting for transfers between devices  21.1 us (21%)
  local copies, waits for them, and re-layouts  6.45 us (6%)
  other arithmetic  5.04 us (5%)
  matrix products  3.09 us (3%)
    ppermute x27, starting transfers between devices, shift(): lax.ppermute(values, axis, [(i, (i + step) % count) for i in range(count)])  38.5 us
    ppermute x27, waiting for transfers between devices, shift(): lax.ppermute(values, axis, [(i, (i + step) % count) for i in range(count)])  21.1 us
    pallas_call x4, Pallas kernels, attend(): pl.pallas_call(functools.partial(attend_kernel, step), out_shape=jax.Shap...  17.9 us
    unnamed x22, local copies, waits for them, and re-layouts  6.15 us
    pallas_call x2, Pallas kernels, project(): pl.pallas_call(kernel, out_shape=(shape, shape), in_specs=[pl.BlockSpec(m...  3.75 us
    dot_general x1, matrix products, body(): jnp.dot(enc_hidden, encoder_down, preferred_element_type=F32).astype(BF16)  3.09 us
  transfers between devices with their start and end apart: 27, of which 11 were waited for; matrix products, arithmetic and copies ran while one was open for 2% of the time, Pallas kernels for 23%

profile of v4, /device:TPU:224, one launch (start us, length us, event | category | flops | bytes accessed | tf_op | source)
XLA Modules:
  0.0 100.2 jit_solution(1395420780428381814)
XLA Ops:
  2.5 3.1 %convolution_convert_fusion = bf16[128,1280]{1,0:T(8,128)(2,1)S(1)} fusion(bf16[640,1280]{1,0:T(8,128)(2,1)S(1)} %copy-done, bf16[1280,640]{1,0:T(8,128)(2,1)} %param.14, bf16[128,1280]{1,0:T(8,128)(2,1)} %param.11, f32[1280]{0:T(1024)} %param.13, f32[1280]{0:T(1024)} %param.12, f32[128]{0:T(128)S(1)} %add_rsqrt_fusion, f32[128]{0:T(128)S(1)} %broadcast_multiply_fusion), kind=kOutput, calls=%fused_computation | convolution fusion | flops 425902080 | bytes 3943424 | tf_op jit(solution)/shard_map/dot_general | solution.py:371
  7.8 2.8 %collective-permute-start.3 = (bf16[64,1280]{1,0:T(8,128)(2,1)}, bf16[64,1280]{1,0:T(8,128)(2,1)}, u32[]{:S(2)}, u32[]{:S(2)}) collective-permute-start(bf16[64,1280]{1,0:T(8,128)(2,1)} %fusion.27), channel_id=1, source_target_pairs={{0,6},{2,0},{4,2},{6,4},{1,7},{3,1},{5,3},{7,5},{8,14},{10,8},{12,... | collective-permute-start | bytes 491528 | tf_op jit(solution)/shard_map/ppermute | solution.py:35
  10.6 2.3 %collective-permute-start.1 = (bf16[64,1280]{1,0:T(8,128)(2,1)}, bf16[64,1280]{1,0:T(8,128)(2,1)}, u32[]{:S(2)}, u32[]{:S(2)}) collective-permute-start(bf16[64,1280]{1,0:T(8,128)(2,1)} %fusion.27), channel_id=1, source_target_pairs={{0,4},{2,6},{4,0},{6,2},{1,5},{3,7},{5,1},{7,3},{8,12},{10,14},{12... | collective-permute-start | bytes 491528 | tf_op jit(solution)/shard_map/ppermute | solution.py:35
  12.9 2.2 %copy-done.1 = bf16[2048,1024]{1,0:T(8,128)(2,1)S(1)} copy-done((bf16[2048,1024]{1,0:T(8,128)(2,1)S(1)}, bf16[2048,1024]{1,0:T(8,128)(2,1)}, u32[]{:S(2)}) %copy-start.1) | copy-done | bytes 4194328
  15.1 2.1 %project.2 = (bf16[4,272,256]{2,1,0:T(8,128)(2,1)}, bf16[4,272,256]{2,1,0:T(8,128)(2,1)S(1)}) custom-call(s32[1]{0:T(128)} %bitcast.2.core, bf16[256,1024]{1,0:T(8,128)(2,1)S(1)} %copy-done.4, f32[1,1024]{1,0:T(1,128)S(1)} %bitcast.18, bf16[2048,1024]{1,0:T(8,128)(2,1)S(1)} %copy-done.1), custom_call_target="tpu_custom_call" | custom-call | tf_op jit(solution)/shard_map/project/pallas_call | solution.py:90
  18.2 3.4 %collective-permute-done.2 = bf16[64,1280]{1,0:T(8,128)(2,1)} collective-permute-done((bf16[64,1280]{1,0:T(8,128)(2,1)}, bf16[64,1280]{1,0:T(8,128)(2,1)}, u32[]{:S(2)}, u32[]{:S(2)}) %collective-permute-start.2) | collective-permute-done | bytes 163872 | tf_op jit(solution)/shard_map/ppermute | solution.py:35
  24.5 2.7 %collective-permute-start.8 = (bf16[272,256]{1,0:T(8,128)(2,1)S(1)}, bf16[272,256]{1,0:T(8,128)(2,1)S(1)}, u32[]{:S(2)}, u32[]{:S(2)}) collective-permute-start(bf16[272,256]{1,0:T(8,128)(2,1)S(1)} %get-tuple-element.48), channel_id=1, source_target_pairs={{0,6},{2,0},{4,2},{6,4},{1,7},{3,1},{5,3},{7,5},{8,14},{10,8},{12,... | collective-permute-start | bytes 417800 | tf_op jit(solution)/shard_map/ppermute | solution.py:35
  27.1 2.2 %copy-done.2 = bf16[2048,1024]{1,0:T(8,128)(2,1)S(1)} copy-done((bf16[2048,1024]{1,0:T(8,128)(2,1)S(1)}, bf16[2048,1024]{1,0:T(8,128)(2,1)}, u32[]{:S(2)}) %copy-start.2) | copy-done | bytes 4194328
  37.0 2.5 %collective-permute-start.12 = (bf16[272,128]{1,0:T(8,128)(2,1)S(1)}, bf16[272,128]{1,0:T(8,128)(2,1)S(1)}, u32[]{:S(2)}, u32[]{:S(2)}) collective-permute-start(bf16[272,128]{1,0:T(8,128)(2,1)S(1)} %get-tuple-element.58), channel_id=1, source_target_pairs={{0,6},{2,0},{4,2},{6,4},{1,7},{3,1},{5,3},{7,5},{8,14},{10,8},{12,... | collective-permute-start | bytes 208904 | tf_op jit(solution)/shard_map/ppermute | solution.py:35
  39.5 2.5 %collective-permute-done.10.refs_5_ = bf16[272,128]{1,0:T(8,128)(2,1)S(1)} collective-permute-done((bf16[272,128]{1,0:T(8,128)(2,1)S(1)}, bf16[272,128]{1,0:T(8,128)(2,1)S(1)}, u32[]{:S(2)}, u32[]{:S(2)}) %collective-permute-start.10) | collective-permute-done | bytes 69664 | tf_op jit(solution)/shard_map/ppermute | solution.py:35
  44.5 2.2 %collective-permute-start.13 = (bf16[272,384]{1,0:T(8,128)(2,1)S(1)}, bf16[272,384]{1,0:T(8,128)(2,1)S(1)}, u32[]{:S(2)}, u32[]{:S(2)}) collective-permute-start(bf16[272,384]{1,0:T(8,128)(2,1)S(1)} %finish_rows.1.refs_0_), channel_id=1, source_target_pairs={{0,32},{32,64},{64,96},{96,128},{128,160},{160,192},{192,224},{224... | collective-permute-start | bytes 626696 | tf_op jit(solution)/shard_map/ppermute | solution.py:35
  46.7 4.8 %collective-permute-done.14.refs_2_ = bf16[272,384]{1,0:T(8,128)(2,1)S(1)} collective-permute-done((bf16[272,384]{1,0:T(8,128)(2,1)S(1)}, bf16[272,384]{1,0:T(8,128)(2,1)S(1)}, u32[]{:S(2)}, u32[]{:S(2)}) %collective-permute-start.14) | collective-permute-done | bytes 208928 | tf_op jit(solution)/shard_map/ppermute | solution.py:35
  51.6 3.2 %collective-permute-start.15 = (bf16[272,384]{1,0:T(8,128)(2,1)S(1)}, bf16[272,384]{1,0:T(8,128)(2,1)S(1)}, u32[]{:S(2)}, u32[]{:S(2)}) collective-permute-start(bf16[272,384]{1,0:T(8,128)(2,1)S(1)} %collective-permute-done.13.refs_1_), channel_id=1, source_target_pairs={{0,32},{32,64},{64,96},{96,128},{128,160},{160,192},{192,224},{224... | collective-permute-start | bytes 626696 | tf_op jit(solution)/shard_map/ppermute | solution.py:35
  55.1 3.1 %collective-permute-start.23 = (bf16[256,512]{1,0:T(8,128)(2,1)S(1)}, bf16[256,512]{1,0:T(8,128)(2,1)}, u32[]{:S(2)}, u32[]{:S(2)}) collective-permute-start(bf16[256,512]{1,0:T(8,128)(2,1)S(1)} %copy-done.7), channel_id=1, source_target_pairs={{0,24},{8,0},{16,8},{24,16},{1,25},{9,1},{17,9},{25,17},{2,26},{10... | collective-permute-start | bytes 786440 | tf_op jit(solution)/shard_map/ppermute | solution.py:35
  58.9 3.2 %collective-permute-start.17 = (bf16[272,384]{1,0:T(8,128)(2,1)S(1)}, bf16[272,384]{1,0:T(8,128)(2,1)S(1)}, u32[]{:S(2)}, u32[]{:S(2)}) collective-permute-start(bf16[272,384]{1,0:T(8,128)(2,1)S(1)} %collective-permute-done.15.refs_3_), channel_id=1, source_target_pairs={{0,32},{32,64},{64,96},{96,128},{128,160},{160,192},{192,224},{224... | collective-permute-start | bytes 626696 | tf_op jit(solution)/shard_map/ppermute | solution.py:35
  63.8 2.1 %collective-permute-done.18.refs_6_ = bf16[272,384]{1,0:T(8,128)(2,1)S(1)} collective-permute-done((bf16[272,384]{1,0:T(8,128)(2,1)S(1)}, bf16[272,384]{1,0:T(8,128)(2,1)S(1)}, u32[]{:S(2)}, u32[]{:S(2)}) %collective-permute-start.18) | collective-permute-done | bytes 208928 | tf_op jit(solution)/shard_map/ppermute | solution.py:35
  66.0 3.3 %collective-permute-start.19 = (bf16[128,384]{1,0:T(8,128)(2,1)S(1)}, bf16[128,384]{1,0:T(8,128)(2,1)S(1)}, u32[]{:S(2)}, u32[]{:S(2)}) collective-permute-start(bf16[128,384]{1,0:T(8,128)(2,1)S(1)} %slice.8), channel_id=1, source_target_pairs={{0,32},{32,64},{64,96},{96,128},{128,160},{160,192},{192,224},{224... | collective-permute-start | bytes 294920 | tf_op jit(solution)/shard_map/ppermute | solution.py:35
  69.4 2.1 %collective-permute-done.19.refs_7_ = bf16[128,384]{1,0:T(8,128)(2,1)S(1)} collective-permute-done((bf16[128,384]{1,0:T(8,128)(2,1)S(1)}, bf16[128,384]{1,0:T(8,128)(2,1)S(1)}, u32[]{:S(2)}, u32[]{:S(2)}) %collective-permute-start.19) | collective-permute-done | bytes 98336 | tf_op jit(solution)/shard_map/ppermute | solution.py:35
  74.0 4.8 %attend.5 = bf16[272,512]{1,0:T(8,128)(2,1)S(1)} custom-call(s32[2]{0:T(128)S(1)} %pad_add_fusion.place, bf16[128,2048]{1,0:T(8,128)(2,1)S(1)} %get-tuple-element.60.keys, bf16[2048,256]{1,0:T(8,128)(2,1)S(1)} %get-tuple-element.61.values, bf16[256,512]{1,0:T(8,128)(2,1)} %collective-permute-done.21.query_ref), custom_call_target="tpu_custom_call" | custom-call | flops 1073741824 | bytes 2097152 | tf_op jit(solution)/shard_map/attend/pallas_call | solution.py:289
  78.9 3.3 %collective-permute-start.22 = (bf16[272,512]{1,0:T(8,128)(2,1)S(1)}, bf16[272,512]{1,0:T(8,128)(2,1)S(1)}, u32[]{:S(2)}, u32[]{:S(2)}) collective-permute-start(bf16[272,512]{1,0:T(8,128)(2,1)S(1)} %attend.5), channel_id=1, source_target_pairs={{0,16},{8,24},{16,0},{24,8},{1,17},{9,25},{17,1},{25,9},{2,18},{10... | collective-permute-start | bytes 835592 | tf_op jit(solution)/shard_map/ppermute | solution.py:35
  82.1 4.6 %attend.6 = bf16[272,512]{1,0:T(8,128)(2,1)S(1)} custom-call(s32[2]{0:T(128)S(1)} %pad_add_fusion.place, bf16[128,2048]{1,0:T(8,128)(2,1)S(1)} %get-tuple-element.60.keys, bf16[2048,256]{1,0:T(8,128)(2,1)S(1)} %get-tuple-element.61.values, bf16[256,512]{1,0:T(8,128)(2,1)} %collective-permute-done.23.query_ref), custom_call_target="tpu_custom_call" | custom-call | flops 1073741824 | bytes 2097152 | tf_op jit(solution)/shard_map/attend/pallas_call | solution.py:289
  87.5 4.2 %attend.7 = bf16[272,512]{1,0:T(8,128)(2,1)S(1)} custom-call(s32[2]{0:T(128)S(1)} %pad_add_fusion.place, bf16[128,2048]{1,0:T(8,128)(2,1)S(1)} %get-tuple-element.60.keys, bf16[2048,256]{1,0:T(8,128)(2,1)S(1)} %get-tuple-element.61.values, bf16[256,512]{1,0:T(8,128)(2,1)S(1)} %collective-permute-done.25.query_ref), custom_call_target="tpu_custom_call" | custom-call | flops 1073741824 | bytes 2097152 | tf_op jit(solution)/shard_map/attend/pallas_call | solution.py:289
  91.7 2.7 %collective-permute-start.26 = (bf16[272,512]{1,0:T(8,128)(2,1)S(1)}, bf16[272,512]{1,0:T(8,128)(2,1)S(1)}, u32[]{:S(2)}, u32[]{:S(2)}) collective-permute-start(bf16[272,512]{1,0:T(8,128)(2,1)S(1)} %attend.7), channel_id=1, source_target_pairs={{0,24},{8,0},{16,8},{24,16},{1,25},{9,1},{17,9},{25,17},{2,26},{10... | collective-permute-start | bytes 835592 | tf_op jit(solution)/shard_map/ppermute | solution.py:35
  94.5 4.3 %attend.4.refs_0_ = bf16[272,512]{1,0:T(8,128)(2,1)S(1)} custom-call(s32[2]{0:T(128)S(1)} %pad_add_fusion.place, bf16[128,2048]{1,0:T(8,128)(2,1)S(1)} %get-tuple-element.60.keys, bf16[2048,256]{1,0:T(8,128)(2,1)S(1)} %get-tuple-element.61.values, bf16[256,512]{1,0:T(8,128)(2,1)S(1)} %copy-done.7), custom_call_target="tpu_custom_call" | custom-call | flops 1073741824 | bytes 2097152 | tf_op jit(solution)/shard_map/attend/pallas_call | solution.py:289
  (80 shorter events, 26.2 us)
Async XLA Ops:
  7.8 10.4 %collective-permute-start.3 = (bf16[64,1280]{1,0:T(8,128)(2,1)}, bf16[64,1280]{1,0:T(8,128)(2,1)}, u32[]{:S(2)}, u32[]{:S(2)}) collective-permute-start(bf16[64,1280]{1,0:T(8,128)(2,1)} %fusion.27), channel_id=1, source_target_pairs={{0,6},{2,0},{4,2},{6,4},{1,7},{3,1},{5,3},{7,5},{8,14},{10,8},{12,... | collective-permute-start | bytes 491528 | tf_op jit(solution)/shard_map/ppermute | solution.py:35
  10.6 11.0 %collective-permute-start.2 = (bf16[64,1280]{1,0:T(8,128)(2,1)}, bf16[64,1280]{1,0:T(8,128)(2,1)}, u32[]{:S(2)}, u32[]{:S(2)}) collective-permute-start(bf16[64,1280]{1,0:T(8,128)(2,1)} %fusion.27), channel_id=1, source_target_pairs={{0,2},{2,4},{4,6},{6,0},{1,3},{3,5},{5,7},{7,1},{8,10},{10,12},{12... | collective-permute-start | bytes 491528 | tf_op jit(solution)/shard_map/ppermute | solution.py:35
  10.6 11.0 %collective-permute-start.1 = (bf16[64,1280]{1,0:T(8,128)(2,1)}, bf16[64,1280]{1,0:T(8,128)(2,1)}, u32[]{:S(2)}, u32[]{:S(2)}) collective-permute-start(bf16[64,1280]{1,0:T(8,128)(2,1)} %fusion.27), channel_id=1, source_target_pairs={{0,4},{2,6},{4,0},{6,2},{1,5},{3,7},{5,1},{7,3},{8,12},{10,14},{12... | collective-permute-start | bytes 491528 | tf_op jit(solution)/shard_map/ppermute | solution.py:35
  17.2 5.8 %collective-permute-start.4 = (bf16[4,272,256]{2,1,0:T(8,128)(2,1)}, bf16[4,272,256]{2,1,0:T(8,128)(2,1)S(1)}, u32[]{:S(2)}, u32[]{:S(2)}) collective-permute-start(bf16[4,272,256]{2,1,0:T(8,128)(2,1)} %get-tuple-element.37), channel_id=1, source_target_pairs={{0,1},{1,0},{2,3},{3,2},{4,5},{5,4},{6,7},{7,6},{8,9},{9,8},{10,11... | collective-permute-start | bytes 1671176 | tf_op jit(solution)/shard_map/ppermute | solution.py:35
  23.2 9.5 %collective-permute-start.6 = (bf16[272,256]{1,0:T(8,128)(2,1)S(1)}, bf16[272,256]{1,0:T(8,128)(2,1)S(1)}, u32[]{:S(2)}, u32[]{:S(2)}) collective-permute-start(bf16[272,256]{1,0:T(8,128)(2,1)S(1)} %get-tuple-element.46), channel_id=1, source_target_pairs={{0,4},{2,6},{4,0},{6,2},{1,5},{3,7},{5,1},{7,3},{8,12},{10,14},{12... | collective-permute-start | bytes 417800 | tf_op jit(solution)/shard_map/ppermute | solution.py:35
  23.9 9.9 %collective-permute-start.7 = (bf16[272,256]{1,0:T(8,128)(2,1)S(1)}, bf16[272,256]{1,0:T(8,128)(2,1)S(1)}, u32[]{:S(2)}, u32[]{:S(2)}) collective-permute-start(bf16[272,256]{1,0:T(8,128)(2,1)S(1)} %get-tuple-element.47), channel_id=1, source_target_pairs={{0,2},{2,4},{4,6},{6,0},{1,3},{3,5},{5,7},{7,1},{8,10},{10,12},{12... | collective-permute-start | bytes 417800 | tf_op jit(solution)/shard_map/ppermute | solution.py:35
  24.5 9.3 %collective-permute-start.8 = (bf16[272,256]{1,0:T(8,128)(2,1)S(1)}, bf16[272,256]{1,0:T(8,128)(2,1)S(1)}, u32[]{:S(2)}, u32[]{:S(2)}) collective-permute-start(bf16[272,256]{1,0:T(8,128)(2,1)S(1)} %get-tuple-element.48), channel_id=1, source_target_pairs={{0,6},{2,0},{4,2},{6,4},{1,7},{3,1},{5,3},{7,5},{8,14},{10,8},{12,... | collective-permute-start | bytes 417800 | tf_op jit(solution)/shard_map/ppermute | solution.py:35
  35.4 6.6 %collective-permute-start.10 = (bf16[272,128]{1,0:T(8,128)(2,1)S(1)}, bf16[272,128]{1,0:T(8,128)(2,1)S(1)}, u32[]{:S(2)}, u32[]{:S(2)}) collective-permute-start(bf16[272,128]{1,0:T(8,128)(2,1)S(1)} %get-tuple-element.56), channel_id=1, source_target_pairs={{0,4},{2,6},{4,0},{6,2},{1,5},{3,7},{5,1},{7,3},{8,12},{10,14},{12... | collective-permute-start | bytes 208904 | tf_op jit(solution)/shard_map/ppermute | solution.py:35
  36.3 6.5 %collective-permute-start.11 = (bf16[272,128]{1,0:T(8,128)(2,1)S(1)}, bf16[272,128]{1,0:T(8,128)(2,1)S(1)}, u32[]{:S(2)}, u32[]{:S(2)}) collective-permute-start(bf16[272,128]{1,0:T(8,128)(2,1)S(1)} %get-tuple-element.57), channel_id=1, source_target_pairs={{0,2},{2,4},{4,6},{6,0},{1,3},{3,5},{5,7},{7,1},{8,10},{10,12},{12... | collective-permute-start | bytes 208904 | tf_op jit(solution)/shard_map/ppermute | solution.py:35
  37.0 5.8 %collective-permute-start.12 = (bf16[272,128]{1,0:T(8,128)(2,1)S(1)}, bf16[272,128]{1,0:T(8,128)(2,1)S(1)}, u32[]{:S(2)}, u32[]{:S(2)}) collective-permute-start(bf16[272,128]{1,0:T(8,128)(2,1)S(1)} %get-tuple-element.58), channel_id=1, source_target_pairs={{0,6},{2,0},{4,2},{6,4},{1,7},{3,1},{5,3},{7,5},{8,14},{10,8},{12,... | collective-permute-start | bytes 208904 | tf_op jit(solution)/shard_map/ppermute | solution.py:35
  43.4 8.2 %collective-permute-start.14 = (bf16[272,384]{1,0:T(8,128)(2,1)S(1)}, bf16[272,384]{1,0:T(8,128)(2,1)S(1)}, u32[]{:S(2)}, u32[]{:S(2)}) collective-permute-start(bf16[272,384]{1,0:T(8,128)(2,1)S(1)} %finish_rows.1.refs_0_), channel_id=1, source_target_pairs={{0,224},{32,0},{64,32},{96,64},{128,96},{160,128},{192,160},{224,1... | collective-permute-start | bytes 626696 | tf_op jit(solution)/shard_map/ppermute | solution.py:35
  44.5 7.1 %collective-permute-start.13 = (bf16[272,384]{1,0:T(8,128)(2,1)S(1)}, bf16[272,384]{1,0:T(8,128)(2,1)S(1)}, u32[]{:S(2)}, u32[]{:S(2)}) collective-permute-start(bf16[272,384]{1,0:T(8,128)(2,1)S(1)} %finish_rows.1.refs_0_), channel_id=1, source_target_pairs={{0,32},{32,64},{64,96},{96,128},{128,160},{160,192},{192,224},{224... | collective-permute-start | bytes 626696 | tf_op jit(solution)/shard_map/ppermute | solution.py:35
  51.6 7.3 %collective-permute-start.16 = (bf16[272,384]{1,0:T(8,128)(2,1)S(1)}, bf16[272,384]{1,0:T(8,128)(2,1)S(1)}, u32[]{:S(2)}, u32[]{:S(2)}) collective-permute-start(bf16[272,384]{1,0:T(8,128)(2,1)S(1)} %collective-permute-done.14.refs_2_), channel_id=1, source_target_pairs={{0,224},{32,0},{64,32},{96,64},{128,96},{160,128},{192,160},{224,1... | collective-permute-start | bytes 626696 | tf_op jit(solution)/shard_map/ppermute | solution.py:35
  51.6 7.3 %collective-permute-start.15 = (bf16[272,384]{1,0:T(8,128)(2,1)S(1)}, bf16[272,384]{1,0:T(8,128)(2,1)S(1)}, u32[]{:S(2)}, u32[]{:S(2)}) collective-permute-start(bf16[272,384]{1,0:T(8,128)(2,1)S(1)} %collective-permute-done.13.refs_1_), channel_id=1, source_target_pairs={{0,32},{32,64},{64,96},{96,128},{128,160},{160,192},{192,224},{224... | collective-permute-start | bytes 626696 | tf_op jit(solution)/shard_map/ppermute | solution.py:35
  55.1 27.0 %collective-permute-start.23 = (bf16[256,512]{1,0:T(8,128)(2,1)S(1)}, bf16[256,512]{1,0:T(8,128)(2,1)}, u32[]{:S(2)}, u32[]{:S(2)}) collective-permute-start(bf16[256,512]{1,0:T(8,128)(2,1)S(1)} %copy-done.7), channel_id=1, source_target_pairs={{0,24},{8,0},{16,8},{24,16},{1,25},{9,1},{17,9},{25,17},{2,26},{10... | collective-permute-start | bytes 786440 | tf_op jit(solution)/shard_map/ppermute | solution.py:35
  58.2 15.8 %collective-permute-start.21 = (bf16[256,512]{1,0:T(8,128)(2,1)S(1)}, bf16[256,512]{1,0:T(8,128)(2,1)}, u32[]{:S(2)}, u32[]{:S(2)}) collective-permute-start(bf16[256,512]{1,0:T(8,128)(2,1)S(1)} %copy-done.7), channel_id=1, source_target_pairs={{0,16},{8,24},{16,0},{24,8},{1,17},{9,25},{17,1},{25,9},{2,18},{10... | collective-permute-start | bytes 786440 | tf_op jit(solution)/shard_map/ppermute | solution.py:35
  58.9 7.0 %collective-permute-start.18 = (bf16[272,384]{1,0:T(8,128)(2,1)S(1)}, bf16[272,384]{1,0:T(8,128)(2,1)S(1)}, u32[]{:S(2)}, u32[]{:S(2)}) collective-permute-start(bf16[272,384]{1,0:T(8,128)(2,1)S(1)} %collective-permute-done.16.refs_4_), channel_id=1, source_target_pairs={{0,224},{32,0},{64,32},{96,64},{128,96},{160,128},{192,160},{224,1... | collective-permute-start | bytes 626696 | tf_op jit(solution)/shard_map/ppermute | solution.py:35
  58.9 7.1 %collective-permute-start.17 = (bf16[272,384]{1,0:T(8,128)(2,1)S(1)}, bf16[272,384]{1,0:T(8,128)(2,1)S(1)}, u32[]{:S(2)}, u32[]{:S(2)}) collective-permute-start(bf16[272,384]{1,0:T(8,128)(2,1)S(1)} %collective-permute-done.15.refs_3_), channel_id=1, source_target_pairs={{0,32},{32,64},{64,96},{96,128},{128,160},{160,192},{192,224},{224... | collective-permute-start | bytes 626696 | tf_op jit(solution)/shard_map/ppermute | solution.py:35
  62.2 25.3 %collective-permute-start.25 = (bf16[256,512]{1,0:T(8,128)(2,1)S(1)}, bf16[256,512]{1,0:T(8,128)(2,1)S(1)}, u32[]{:S(2)}, u32[]{:S(2)}) collective-permute-start(bf16[256,512]{1,0:T(8,128)(2,1)S(1)} %copy-done.7), channel_id=1, source_target_pairs={{0,8},{8,16},{16,24},{24,0},{1,9},{9,17},{17,25},{25,1},{2,10},{10... | collective-permute-start | bytes 786440 | tf_op jit(solution)/shard_map/ppermute | solution.py:35
  65.9 6.0 %collective-permute-start.20 = (bf16[144,384]{1,0:T(8,128)(2,1)S(1)}, bf16[144,384]{1,0:T(8,128)(2,1)S(1)}, u32[]{:S(2)}, u32[]{:S(2)}) collective-permute-start(bf16[144,384]{1,0:T(8,128)(2,1)S(1)} %slice.9), channel_id=1, source_target_pairs={{0,224},{32,0},{64,32},{96,64},{128,96},{160,128},{192,160},{224,1... | collective-permute-start | bytes 331784 | tf_op jit(solution)/shard_map/ppermute | solution.py:35
  66.0 5.5 %collective-permute-start.19 = (bf16[128,384]{1,0:T(8,128)(2,1)S(1)}, bf16[128,384]{1,0:T(8,128)(2,1)S(1)}, u32[]{:S(2)}, u32[]{:S(2)}) collective-permute-start(bf16[128,384]{1,0:T(8,128)(2,1)S(1)} %slice.8), channel_id=1, source_target_pairs={{0,32},{32,64},{64,96},{96,128},{128,160},{160,192},{192,224},{224... | collective-permute-start | bytes 294920 | tf_op jit(solution)/shard_map/ppermute | solution.py:35
  78.9 19.9 %collective-permute-start.22 = (bf16[272,512]{1,0:T(8,128)(2,1)S(1)}, bf16[272,512]{1,0:T(8,128)(2,1)S(1)}, u32[]{:S(2)}, u32[]{:S(2)}) collective-permute-start(bf16[272,512]{1,0:T(8,128)(2,1)S(1)} %attend.5), channel_id=1, source_target_pairs={{0,16},{8,24},{16,0},{24,8},{1,17},{9,25},{17,1},{25,9},{2,18},{10... | collective-permute-start | bytes 835592 | tf_op jit(solution)/shard_map/ppermute | solution.py:35
  86.8 12.0 %collective-permute-start.24 = (bf16[272,512]{1,0:T(8,128)(2,1)S(1)}, bf16[272,512]{1,0:T(8,128)(2,1)S(1)}, u32[]{:S(2)}, u32[]{:S(2)}) collective-permute-start(bf16[272,512]{1,0:T(8,128)(2,1)S(1)} %attend.6), channel_id=1, source_target_pairs={{0,8},{8,16},{16,24},{24,0},{1,9},{9,17},{17,25},{25,1},{2,10},{10... | collective-permute-start | bytes 835592 | tf_op jit(solution)/shard_map/ppermute | solution.py:35
  91.7 7.0 %collective-permute-start.26 = (bf16[272,512]{1,0:T(8,128)(2,1)S(1)}, bf16[272,512]{1,0:T(8,128)(2,1)S(1)}, u32[]{:S(2)}, u32[]{:S(2)}) collective-permute-start(bf16[272,512]{1,0:T(8,128)(2,1)S(1)} %attend.7), channel_id=1, source_target_pairs={{0,24},{8,0},{16,8},{24,16},{1,25},{9,1},{17,9},{25,17},{2,26},{10... | collective-permute-start | bytes 835592 | tf_op jit(solution)/shard_map/ppermute | solution.py:35
  (14 other events, 102.4 us)
